TPU v7x, 32 devices: a whole 2x2x4 slice. The times are simulated.
32 devices in a mesh: epoch: 2 (over x), tile: 16 (over z, y, core).
Axes of the slice: x: 2, y: 2, z: 4, core: 2. Of those that a mesh axis runs over, the one named last changes fastest.
Arguments:
- owners: int32 [2, 2048], P('epoch', 'tile'), may hold values from 0 to 15, as said below
- row_offsets: int32 [2, 2048], P('epoch', 'tile'), may hold values from 0 to 224
- col_offsets: int32 [2, 2048], P('epoch', 'tile'), may hold values from 0 to 4064
- samples: bfloat16 [2, 2048, 2, 256], P('epoch', 'tile'), may hold values from -6 to 6
- coords: float32 [2, 2048, 2, 256], P('epoch', 'tile'), may hold values from 4 to 28
- taper_rows: float32 [16, 256], P('epoch'), may hold values from 1 to 4
- taper_cols: float32 [4096], P('tile'), may hold values from 1 to 4
Outputs:
- image: float32 [16, 256, 4096], P('epoch', None, 'tile')
Inputs may be any that keep to these rules, and one draw needn't show every extreme that they name: `owners`: in every epoch, within each aligned block of 128 slots (the slots of one index of tile), no owner tile is named more than 10 times, and one owner tile is named exactly 10 times in every block of that epoch.
All inputs are finite; a program needn't handle non-finite values.
Results may differ from a plain program's by a relative error of at most 0.0053.
Values may be sent and summed in bfloat16 or wider, within the bound.
A program may use at most 128 MiB of HBM per device.

v0:
```python
import functools
import math

import jax
import jax.numpy as jnp
import numpy as np
from jax import lax
from jax.experimental import pallas as pl
from jax.experimental.pallas import tpu as pltpu
from jax.sharding import PartitionSpec as P

SUB = 32
LANES = 128
VMEM_BYTES = 56 * 1024 * 1024


def kernel_weights(distance):
    return jnp.square(jnp.maximum(1.0 - jnp.square(distance * 0.25), 0.0))


def fourier(values):
    count = len(values)
    if count == 1:
        return values
    if count == 2:
        (ar, ai), (br, bi) = values
        return [(ar + br, ai + bi), (ar - br, ai - bi)]
    even, odd = fourier(values[0::2]), fourier(values[1::2])
    low, high = [], []
    for k in range(count // 2):
        (er, ei), (orr, oi) = even[k], odd[k]
        if k == 0:
            tr, ti = orr, oi
        elif 4 * k == count:
            tr, ti = -oi, orr
        elif 8 * k == count:
            s = math.sqrt(0.5)
            tr, ti = (orr - oi) * s, (orr + oi) * s
        elif 8 * k == 3 * count:
            s = math.sqrt(0.5)
            tr, ti = (orr + oi) * -s, (orr - oi) * s
        else:
            c, s = math.cos(2 * math.pi * k / count), math.sin(2 * math.pi * k / count)
            tr, ti = orr * c - oi * s, orr * s + oi * c
        low.append((er + tr, ei + ti))
        high.append((er - tr, ei - ti))
    return low + high


def grid_kernel(
    pairs, tile_count, epoch_count, src_ref, data_ref, info_ref, got_ref, others_ref, *scratch
):
    packed, t_send, t_recv, x_send, x_recv = scratch
    me, epoch = lax.axis_index("tile"), lax.axis_index("epoch")
    mesh_id = pl.DeviceIdType.MESH
    cells = lax.broadcasted_iota(jnp.int32, (SUB, data_ref.shape[2]), 0).astype(jnp.float32)

    barrier = pltpu.get_barrier_semaphore()

    def greet(k, carry):
        peer = lax.rem(me + k, tile_count)
        pl.semaphore_signal(barrier, inc=1, device_id={"tile": peer}, device_id_type=mesh_id)
        return carry

    lax.fori_loop(1, tile_count, greet, 0)
    for k in range(1, epoch_count):
        peer = lax.rem(epoch + k, epoch_count)
        pl.semaphore_signal(barrier, inc=1, device_id={"epoch": peer}, device_id_type=mesh_id)
    pl.semaphore_wait(barrier, tile_count + epoch_count - 2)

    def one(slot):
        data = data_ref[slot]
        along_u = kernel_weights(cells - data[0:1]).astype(jnp.bfloat16)
        along_v = kernel_weights(cells - data[1:2])
        weighted = jnp.concatenate([data[2:3] * along_v, data[3:4] * along_v], 0)
        return lax.dot_general(
            along_u,
            weighted.astype(jnp.bfloat16),
            (((1,), (1,)), ((), ())),
            preferred_element_type=jnp.float32,
        )

    def make(tile, out_ref):
        for k in range(pairs):
            at = (tile * pairs + k) * 2
            both = jnp.concatenate([one(src_ref[at]), one(src_ref[at + 1])], 1)
            out_ref[tile, k * SUB : (k + 1) * SUB, :] = both.astype(jnp.bfloat16)
        out_ref[tile, pairs * SUB :, :] = info_ref[tile]

    def tile_copy(k):
        peer = lax.rem(me + k, tile_count)
        return pltpu.make_async_remote_copy(
            src_ref=packed.at[peer],
            dst_ref=got_ref.at[me],
            send_sem=t_send.at[k],
            recv_sem=t_recv.at[k],
            device_id={"tile": peer},
            device_id_type=mesh_id,
        )

    def epoch_copy(k, j):
        origin = lax.rem(me + tile_count - k, tile_count)
        return pltpu.make_async_remote_copy(
            src_ref=got_ref.at[origin],
            dst_ref=others_ref.at[(j - 1) * tile_count + origin],
            send_sem=x_send.at[(j - 1) * tile_count + k],
            recv_sem=x_recv.at[(j - 1) * tile_count + k],
            device_id={"epoch": lax.rem(epoch + j, epoch_count)},
            device_id_type=mesh_id,
        )

    def send(k, carry):
        make(lax.rem(me + k, tile_count), packed)
        tile_copy(k).start()
        return carry

    make(me, got_ref)
    for j in range(1, epoch_count):
        epoch_copy(0, j).start()
    lax.fori_loop(1, tile_count, send, 0)

    def forward(k, carry):
        tile_copy(k).wait_recv()
        for j in range(1, epoch_count):
            epoch_copy(k, j).start()
        return carry

    lax.fori_loop(1, tile_count, forward, 0)

    def sent_all(k, carry):
        tile_copy(k).wait_send()
        return carry

    lax.fori_loop(1, tile_count, sent_all, 0)

    def crossed(k, carry):
        for j in range(1, epoch_count):
            epoch_copy(k, j).wait()
        return carry

    lax.fori_loop(0, tile_count, crossed, 0)


def add_slots(pairs, row_ref, block_ref, start_ref, weight_ref, pool_ref, acc):
    lane_blocks, acc_rows = acc.shape[1], acc.shape[2]

    def clear(i, carry):
        acc[0, i] = jnp.zeros((acc_rows, LANES), jnp.float32)
        acc[1, i] = jnp.zeros((acc_rows, LANES), jnp.float32)
        return carry

    lax.fori_loop(0, lane_blocks, clear, 0)
    shape = (SUB, 2 * LANES)
    steps = lax.broadcasted_iota(jnp.int32, shape, 1) - lax.broadcasted_iota(jnp.int32, shape, 0)

    def per_source(g, carry):
        windows = []
        weight = weight_ref[g]
        for k in range(pairs):
            block = pool_ref[g, k * SUB : (k + 1) * SUB, :]
            for j in range(2):
                start = start_ref[(g * pairs + k) * 2 + j]
                select = jnp.where(steps == start, 1.0, 0.0).astype(jnp.bfloat16)
                parts = jnp.concatenate(
                    [block[:, (2 * j + p) * SUB : (2 * j + p + 1) * SUB] for p in range(2)], 0
                )
                windows.append(jnp.dot(parts, select, preferred_element_type=jnp.float32) * weight)
        for i, window in enumerate(windows):
            at = g * pairs * 2 + i
            row, lane_block = row_ref[at], block_ref[at]
            for p in range(2):
                for h in range(2):
                    acc[p, lane_block + h, pl.ds(row, SUB), :] += window[
                        p * SUB : (p + 1) * SUB, h * LANES : (h + 1) * LANES
                    ]
        return carry

    lax.fori_loop(0, pool_ref.shape[0], per_source, 0)


def place_kernel(pairs, row_ref, block_ref, start_ref, weight_ref, pool_ref, band_ref, acc):
    add_slots(pairs, row_ref, block_ref, start_ref, weight_ref, pool_ref, acc)
    rows_out = band_ref.shape[2]

    def put(i, carry):
        for p in range(2):
            band_ref[p, i] = acc[p, i, SUB : SUB + rows_out, :].astype(jnp.bfloat16)
        return carry

    lax.fori_loop(0, band_ref.shape[1], put, 0)


def rows_kernel(
    pairs,
    row_ref,
    block_ref,
    start_ref,
    weight_ref,
    pool_ref,
    band_ref,
    cos_ref,
    sin_ref,
    second_ref,
    *rest,
):
    out_refs, (acc, turned_ref) = rest[:-2], rest[-2:]
    add_slots(pairs, row_ref, block_ref, start_ref, weight_ref, pool_ref, acc)
    tile_count, rows_out, wide = turned_ref.shape
    block_len = wide // 2
    group = min(16, rows_out)
    width = min(LANES, block_len)

    def per_group(i, carry):
        for h in range(block_len // width):
            values = []
            for a in range(tile_count):
                first = a * block_len + h * width
                lane, at = first % LANES, first // LANES
                values.append(
                    tuple(
                        acc[p, at, pl.ds(SUB + i * group, group), lane : lane + width]
                        + band_ref[p, at, pl.ds(i * group, group), lane : lane + width].astype(
                            jnp.float32
                        )
                        for p in range(2)
                    )
                )
            lanes = slice(h * width, (h + 1) * width)
            for m, (re, im) in enumerate(fourier(values)):
                c, s = cos_ref[m : m + 1, lanes], sin_ref[m : m + 1, lanes]
                turned = (re * c - im * s, re * s + im * c)
                for p in range(2):
                    first = p * block_len + h * width
                    turned_ref[m, pl.ds(i * group, group), first : first + width] = turned[
                        p
                    ].astype(jnp.bfloat16)
        return carry

    lax.fori_loop(0, rows_out // group, per_group, 0)

    def per_tile(m, carry):
        moved = jnp.dot(turned_ref[m], second_ref[...], preferred_element_type=jnp.float32)
        for j, out_ref in enumerate(out_refs):
            out_ref[m] = moved[:, j * 2 * width : (j + 1) * 2 * width].astype(jnp.bfloat16)
        return carry

    lax.fori_loop(0, tile_count, per_tile, 0)


def columns_kernel(tile_count, epoch_count, chunks, *refs):
    sent, last_ref, outs = refs[:chunks], refs[chunks], refs[chunks + 1 : 2 * chunks + 1]
    got, mixed, share, landed, t_send, t_recv, x_send, x_recv, own_sem = refs[2 * chunks + 1 :]
    rows_here, width = got.shape[2], got.shape[3] // 2
    kept = tile_count // epoch_count
    me, epoch = lax.axis_index("tile"), lax.axis_index("epoch")
    mesh_id = pl.DeviceIdType.MESH

    barrier = pltpu.get_barrier_semaphore()

    def greet(k, carry):
        peer = lax.rem(me + k, tile_count)
        pl.semaphore_signal(barrier, inc=1, device_id={"tile": peer}, device_id_type=mesh_id)
        return carry

    lax.fori_loop(1, tile_count, greet, 0)
    for k in range(1, epoch_count):
        peer = lax.rem(epoch + k, epoch_count)
        pl.semaphore_signal(barrier, inc=1, device_id={"epoch": peer}, device_id_type=mesh_id)
    pl.semaphore_wait(barrier, tile_count + epoch_count - 2)

    def tile_copy(j, k):
        peer = lax.rem(me + k, tile_count)
        return pltpu.make_async_remote_copy(
            src_ref=sent[j].at[peer],
            dst_ref=got.at[j, me],
            send_sem=t_send.at[j * tile_count + k],
            recv_sem=t_recv.at[j * tile_count + k],
            device_id={"tile": peer},
            device_id_type=mesh_id,
        )

    def epoch_copy(j, k, c):
        at = (j * (epoch_count - 1) + k - 1) * kept + c
        return pltpu.make_async_remote_copy(
            src_ref=share.at[j, k - 1, c],
            dst_ref=landed.at[j, k - 1, c],
            send_sem=x_send.at[at],
            recv_sem=x_recv.at[at],
            device_id={"epoch": lax.rem(epoch + k, epoch_count)},
            device_id_type=mesh_id,
        )

    def own_copy(j):
        return pltpu.make_async_copy(sent[j].at[me], got.at[j, me], own_sem.at[j])

    for j in range(chunks):

        def send(k, carry, j=j):
            tile_copy(j, k).start()
            return carry

        lax.fori_loop(1, tile_count, send, 0)
        own_copy(j).start()

    group = min(16, rows_here)
    for j in range(chunks):

        def receive(k, carry, j=j):
            tile_copy(j, k).wait_recv()
            return carry

        lax.fori_loop(1, tile_count, receive, 0)
        own_copy(j).wait()

        def per_group(i, carry, j=j):
            values = [
                tuple(
                    got[
                        j, t, pl.ds(i * group, group), p * width : (p + 1) * width
                    ].astype(jnp.float32)
                    for p in range(2)
                )
                for t in range(tile_count)
            ]
            for c, parts in enumerate(fourier(values)):
                for p in range(2):
                    mixed[c, pl.ds(p * rows_here + i * group, group), :] = parts[p].astype(
                        jnp.bfloat16
                    )
            return carry

        lax.fori_loop(0, rows_here // group, per_group, 0)

        for k in range(1, epoch_count):
            first = lax.rem(epoch + k, epoch_count) * kept

            def away(c, carry, j=j, k=k, first=first):
                share[j, k - 1, c] = jnp.dot(
                    last_ref[first + c], mixed[first + c], preferred_element_type=jnp.float32
                ).astype(jnp.bfloat16)
                epoch_copy(j, k, c).start()
                return carry

            lax.fori_loop(0, kept, away, 0)

        def home(c, carry, j=j):
            outs[j][c] = jnp.dot(
                last_ref[epoch * kept + c],
                mixed[epoch * kept + c],
                preferred_element_type=jnp.float32,
            )
            return carry

        lax.fori_loop(0, kept, home, 0)

    for j in range(chunks):

        def sent_all(k, carry, j=j):
            tile_copy(j, k).wait_send()
            return carry

        lax.fori_loop(1, tile_count, sent_all, 0)
        for k in range(1, epoch_count):

            def add(c, carry, j=j, k=k):
                epoch_copy(j, k, c).wait()
                outs[j][c] += landed[j, k - 1, c].astype(jnp.float32)
                return carry

            lax.fori_loop(0, kept, add, 0)


def turns(product, modulus):
    angles = (product % modulus) * (2.0 * math.pi / modulus)
    return np.cos(angles), np.sin(angles)


def make_tables(tile_count, epoch_count, block_len):
    grid_size = tile_count * block_len
    long_idx = np.arange(block_len)
    tile_idx = np.arange(tile_count)
    turn_cos, turn_sin = turns(tile_idx[:, None] * long_idx[None, :], grid_size)
    c, s = turns(long_idx[:, None] * long_idx[None, :], block_len)
    second = np.stack([np.stack([c, s], 1), np.stack([-s, c], 1)], 0)
    width = min(LANES, block_len)
    second = second.reshape(2 * block_len, 2, block_len // width, width)
    second = second.transpose(0, 2, 1, 3).reshape(2 * block_len, 2 * block_len)
    rows_here = block_len // epoch_count
    row = np.arange(block_len).reshape(epoch_count, 1, 1, rows_here)
    pixel = (long_idx[None, :] * tile_count + tile_idx[:, None])[None, :, :, None]
    c, s = turns(row * pixel, grid_size)
    last = np.concatenate([c, -s], -1)
    return (
        turn_cos.astype(np.float32),
        turn_sin.astype(np.float32),
        second.astype(jnp.bfloat16),
        last.astype(jnp.bfloat16),
    )


def vmem(count):
    return [pl.BlockSpec(memory_space=pltpu.VMEM)] * count


def smem(count):
    return [pl.BlockSpec(memory_space=pltpu.SMEM)] * count


def body(tables, owners, row_offsets, col_offsets, samples, coords, taper_rows, taper_cols):
    tile_count = lax.axis_size("tile")
    epoch_count = lax.axis_size("epoch")
    epoch_index = lax.axis_index("epoch")
    slot_owner = owners[0]
    n_slots = slot_owner.shape[0]
    pairs = (max(2, n_slots * 5 // (4 * tile_count)) + 1) // 2
    capacity = 2 * pairs
    info_rows = -(-capacity // 16) * 16
    block_rows = pairs * SUB + info_rows
    block_len = taper_cols.shape[0]
    rows_here = block_len // epoch_count
    params = pltpu.CompilerParams(vmem_limit_bytes=VMEM_BYTES)
    turn_cos, turn_sin, second, last = tables

    slot_idx = jnp.arange(n_slots, dtype=jnp.int32)
    same_before = (slot_owner[:, None] == slot_owner[None, :]) & (
        slot_idx[None, :] < slot_idx[:, None]
    )
    slot_rank = jnp.sum(same_before.astype(jnp.int32), 1)
    hit = (slot_owner[None, None, :] == jnp.arange(tile_count, dtype=jnp.int32)[:, None, None]) & (
        slot_rank[None, None, :] == jnp.arange(info_rows, dtype=jnp.int32)[None, :, None]
    )
    fields = [
        jnp.sum(jnp.where(hit, f, 0), 2)
        for f in (
            jnp.ones_like(slot_owner),
            row_offsets[0],
            col_offsets[0] // LANES,
            col_offsets[0] % LANES,
            slot_idx,
        )
    ]
    source = fields[4][:, :capacity].reshape(-1)
    info = jnp.pad(jnp.stack(fields[:4], -1), ((0, 0), (0, 0), (0, LANES - 4))).astype(jnp.bfloat16)
    data = jnp.concatenate([coords[0], samples[0].astype(jnp.float32)], 1)

    tile_sems = pltpu.SemaphoreType.DMA((tile_count,))
    epoch_sems = pltpu.SemaphoreType.DMA(((epoch_count - 1) * tile_count,))
    got, others = pl.pallas_call(
        functools.partial(grid_kernel, pairs, tile_count, epoch_count),
        out_shape=[
            jax.ShapeDtypeStruct((n * tile_count, block_rows, LANES), jnp.bfloat16)
            for n in (1, epoch_count - 1)
        ],
        in_specs=smem(1) + vmem(2),
        out_specs=vmem(2),
        scratch_shapes=[
            pltpu.VMEM((tile_count, block_rows, LANES), jnp.bfloat16),
            tile_sems,
            tile_sems,
            epoch_sems,
            epoch_sems,
        ],
        compiler_params=pltpu.CompilerParams(
            vmem_limit_bytes=VMEM_BYTES, collective_id=1, has_side_effects=True
        ),
        name="grid_slots",
    )(source, data, info)
    spare = rows_here + 2 * SUB
    lane_blocks = tile_count * block_len // LANES

    def places(pool):
        table = pool[:, pairs * SUB : pairs * SUB + capacity, :4].astype(jnp.int32)
        valid = table[:, :, 0] > 0
        counts = jnp.sum(table[:, :, 0].reshape(-1, tile_count * capacity), 1)
        weight = jnp.repeat(1.0 / jnp.maximum(counts, 1).astype(jnp.float32), tile_count)
        first_row = table[:, :, 1] - epoch_index * rows_here + SUB
        inside = valid & (first_row > 0) & (first_row < rows_here + SUB)
        place_row = jnp.where(inside, first_row, spare).reshape(-1)
        return place_row, table[:, :, 2].reshape(-1), table[:, :, 3].reshape(-1), weight, pool

    acc = pltpu.VMEM((2, lane_blocks + 1, spare + SUB, LANES), jnp.float32)
    band = pl.pallas_call(
        functools.partial(place_kernel, pairs),
        out_shape=jax.ShapeDtypeStruct((2, lane_blocks, rows_here, LANES), jnp.bfloat16),
        in_specs=smem(4) + vmem(1),
        out_specs=vmem(1)[0],
        scratch_shapes=[acc],
        compiler_params=params,
        cost_estimate=pl.CostEstimate(flops=8 * 10**9, bytes_accessed=10**7, transcendentals=0),
        name="place_subgrids",
    )(*places(got))

    width = min(LANES, block_len)
    chunks = block_len // width
    sent = pl.pallas_call(
        functools.partial(rows_kernel, pairs),
        out_shape=[
            jax.ShapeDtypeStruct((tile_count, rows_here, 2 * width), jnp.bfloat16)
            for _ in range(chunks)
        ],
        in_specs=smem(4) + vmem(5),
        out_specs=vmem(chunks),
        scratch_shapes=[acc, pltpu.VMEM((tile_count, rows_here, 2 * block_len), jnp.bfloat16)],
        compiler_params=params,
        name="row_sections",
    )(*places(others), band, jnp.asarray(turn_cos), jnp.asarray(turn_sin), jnp.asarray(second))

    last_here = lax.dynamic_index_in_dim(jnp.asarray(last), epoch_index, 0, keepdims=False)
    kept = tile_count // epoch_count
    shares_shape = (chunks, epoch_count - 1, kept, block_len, width)
    tile_sems = pltpu.SemaphoreType.DMA((chunks * tile_count,))
    epoch_sems = pltpu.SemaphoreType.DMA((chunks * (epoch_count - 1) * kept,))
    sums = pl.pallas_call(
        functools.partial(columns_kernel, tile_count, epoch_count, chunks),
        out_shape=[
            jax.ShapeDtypeStruct((kept, block_len, width), jnp.float32) for _ in range(chunks)
        ],
        in_specs=vmem(chunks + 1),
        out_specs=vmem(chunks),
        scratch_shapes=[
            pltpu.VMEM((chunks, tile_count, rows_here, 2 * width), jnp.bfloat16),
            pltpu.VMEM((tile_count, 2 * rows_here, width), jnp.bfloat16),
            pltpu.VMEM(shares_shape, jnp.bfloat16),
            pltpu.VMEM(shares_shape, jnp.bfloat16),
            tile_sems,
            tile_sems,
            epoch_sems,
            epoch_sems,
            pltpu.SemaphoreType.DMA((chunks,)),
        ],
        compiler_params=pltpu.CompilerParams(
            vmem_limit_bytes=VMEM_BYTES, collective_id=0, has_side_effects=True
        ),
        name="columns",
    )(*sent, last_here)
    image_sum = jnp.concatenate(sums, 2)
    image_scale = math.sqrt(n_slots) / (64.0 * tile_count * math.sqrt(epoch_count))
    return image_sum * (image_scale * taper_rows)[:, :, None] * taper_cols[None, None, :]


def solution(mesh):
    placed = (
        P("epoch", "tile"),
        P("epoch", "tile"),
        P("epoch", "tile"),
        P("epoch", "tile", None, None),
        P("epoch", "tile", None, None),
        P("epoch", None),
        P("tile"),
    )

    def whole(owners, row_offsets, col_offsets, samples, coords, taper_rows, taper_cols):
        tables = make_tables(
            mesh.shape["tile"], mesh.shape["epoch"], taper_cols.shape[0] // mesh.shape["tile"]
        )
        return jax.shard_map(
            functools.partial(body, tables),
            mesh=mesh,
            in_specs=placed,
            out_specs=P("epoch", None, "tile"),
            check_vma=False,
        )(owners, row_offsets, col_offsets, samples, coords, taper_rows, taper_cols)

    return whole
```

profile of v0, /device:TPU:31, one launch (start us, length us, event | category | flops | bytes accessed | tf_op | source)
XLA Modules:
  0.0 152.0 jit_solution(600791290061645399)
XLA Ops:
  0.0 0.9 convert_reduce_fusion
  0.9 0.7 iota_compare_fusion.2
  1.6 0.7 and_select_fusion.8
  2.2 2.1 %fusion.2 = (s32[16,16]{1,0:T(8,128)S(1)}, s32[16,16]{1,0:T(8,128)S(1)}, s32[16,16]{1,0:T(8,128)S(1)}, s32[16,16]{1,0:T(8,128)S(1)}, s32[16,16]{1,0:T(8,128)S(1)}) fusion(pred[16,128]{1,0:T(8,128)(4,1)S(1)} %iota_compare_fusion.1, pred[16,128]{1,0:T(8,128)(4,1)S(1)} %iota_compare_fusion.2, s32[128]{0:T(128)S(1)} %get-tuple-element.31, ...), kind=kLoop, calls=%fused_computation.10 | loop fusion | flops 359168 | bytes 10752 | tf_op jit(solution)/shard_map/reduce_sum | solution.py:433
  4.4 0.2 copy.17
  4.6 0.6 pad.5.info_ref
  5.2 0.7 reshape.96.src_ref
  5.9 1.0 bitcast_convert_fusion
  6.9 2.0 %pad_maximum_fusion.data_ref = f32[128,4,256]{2,1,0:T(4,128)} fusion(f32[128,2,256]{2,1,0:T(2,128)S(1)} %bitcast_convert_fusion, f32[128,2,256]{2,1,0:T(2,128)} %bitcast.32), kind=kLoop, calls=%fused_computation.3 | loop fusion | flops 131072 | bytes 1048576 | tf_op jit(solution)/shard_map/concatenate | solution.py:444
  8.9 31.0 %grid_slots.1 = (bf16[16,176,128]{2,1,0:T(8,128)(2,1)}, bf16[16,176,128]{2,1,0:T(8,128)(2,1)}) custom-call(s32[160]{0:T(256)} %reshape.96.src_ref, f32[128,4,256]{2,1,0:T(4,128)} %pad_maximum_fusion.data_ref, bf16[16,16,128]{2,1,0:T(8,128)(2,1)} %pad.5.info_ref), custom_call_target="tpu_custom_call" | custom-call | tf_op jit(solution)/shard_map/grid_slots/pallas_call | solution.py:448
  39.8 0.9 slice_convert_fusion
  40.7 1.6 %slice_reduce_fusion.4 = (s32[]{:T(128)}, s32[16,10]{1,0:T(8,128)S(1)}, s32[16,10]{1,0:T(8,128)S(1)}, s32[16,10]{1,0:T(8,128)S(1)}) fusion(s32[16,10,4]{2,1,0:T(8,128)S(1)} %slice_convert_fusion, s32[]{:T(128)S(6)} %mul.26), kind=kLoop, calls=%fused_computation.27 | loop fusion | flops 479 | bytes 4488 | tf_op jit(solution)/shard_map/reduce_sum | solution.py:474
  42.3 0.1 add.31
  42.4 0.4 compare_reduce_fusion
  42.7 0.1 gt.26
  42.8 0.6 and_select_fusion.5.row_ref
  44.1 0.5 reshape.98.weight_ref
  44.6 0.7 reshape_squeeze.16.block_ref
  45.2 0.7 reshape_squeeze.17.start_ref
  45.9 8.8 %place_subgrids.1.band_ref = bf16[2,32,128,128]{3,2,1,0:T(8,128)(2,1)} custom-call(s32[160]{0:T(256)} %and_select_fusion.5.row_ref, s32[160]{0:T(256)} %reshape_squeeze.16.block_ref, s32[160]{0:T(256)} %reshape_squeeze.17.start_ref, f32[16]{0:T(128)} %reshape.98.weight_ref, bf16[16,176,128]{2,1,0:T(8,128)(2,1)} %get-tuple-element.12.pool_ref), custom_call_target="tpu_custom_call" | custom-call | flops 8000000000 | bytes 10000000 | tf_op jit(solution)/shard_map/place_subgrids/pallas_call | solution.py:482
  54.7 0.9 slice_convert_fusion.1
  55.6 1.6 %slice_reduce_fusion.5 = (s32[]{:T(128)}, s32[16,10]{1,0:T(8,128)S(1)}, s32[16,10]{1,0:T(8,128)S(1)}, s32[16,10]{1,0:T(8,128)S(1)}) fusion(s32[16,10,4]{2,1,0:T(8,128)S(1)} %slice_convert_fusion.1, s32[]{:T(128)S(6)} %mul.26), kind=kLoop, calls=%fused_computation.28 | loop fusion | flops 479 | bytes 4488 | tf_op jit(solution)/shard_map/reduce_sum | solution.py:474
  57.3 0.4 compare_reduce_fusion.1
  57.7 0.1 gt.23
  57.8 0.6 and_select_fusion.6.row_ref
  59.1 0.5 reshape.97.weight_ref
  59.6 0.6 reshape_squeeze.14.block_ref
  60.2 0.6 reshape_squeeze.15.start_ref
  60.9 15.2 %row_sections.1 = (bf16[16,128,256]{2,1,0:T(8,128)(2,1)}, bf16[16,128,256]{2,1,0:T(8,128)(2,1)}) custom-call(s32[160]{0:T(256)} %and_select_fusion.6.row_ref, s32[160]{0:T(256)} %reshape_squeeze.14.block_ref, s32[160]{0:T(256)} %reshape_squeeze.15.start_ref, f32[16]{0:T(128)} %reshape.97.weight_ref, bf16[16,176,128]{2,1,0:T(8,128)(2,1)} %get-tuple-element.11.pool_ref, ...), custom_call_target="tpu_custom_call" | custom-call | tf_op jit(solution)/shard_map/row_sections/pallas_call | solution.py:495
  76.1 3.1 %dynamic-slice_bitcast_fusion.refs_2_ = bf16[16,256,256]{2,1,0:T(8,128)(2,1)} fusion(bf16[2,16,256,256]{3,2,1,0:T(8,128)(2,1)} %constant.70.clone, s32[]{:T(128)S(6)} %select_n.50), kind=kLoop, calls=%fused_computation.2 | loop fusion | bytes 4194308 | tf_op jit(solution)/shard_map/jit(dynamic_index_in_dim)/squeeze | solution.py:508
  79.2 69.6 %columns.1 = (f32[8,256,128]{2,1,0:T(8,128)}, f32[8,256,128]{2,1,0:T(8,128)}) custom-call(bf16[16,128,256]{2,1,0:T(8,128)(2,1)} %get-tuple-element.13.refs_0_, bf16[16,128,256]{2,1,0:T(8,128)(2,1)} %get-tuple-element.14.refs_1_, bf16[16,256,256]{2,1,0:T(8,128)(2,1)} %dynamic-slice_bitcast_fusion.refs_2_), custom_call_target="tpu_custom_call" | custom-call | tf_op jit(solution)/shard_map/columns/pallas_call | solution.py:513
  148.8 3.2 %fusion = f32[8,256,256]{2,1,0:T(8,128)} fusion(f32[8,256,128]{2,1,0:T(8,128)} %get-tuple-element.16, f32[8,256,128]{2,1,0:T(8,128)} %get-tuple-element.15, f32[256]{0:T(256)S(1)} %copy-done.1, f32[8,256]{1,0:T(8,128)S(1)} %broadcast_multiply_fusion), kind=kLoop, calls=%fused_computation.1 | loop fusion | flops 1572864 | bytes 4203520 | tf_op jit(solution)/shard_map/mul | solution.py:538
  (10 shorter events, 0.1 us)
Async XLA Ops:
  79.2 69.6 %copy-start = (f32[8,256]{1,0:T(8,128)S(1)}, f32[8,256]{1,0:T(8,128)}, u32[]{:S(2)}) copy-start(f32[8,256]{1,0:T(8,128)} %param.16) | copy-start | bytes 24580
  79.2 69.6 %copy-start.1 = (f32[256]{0:T(256)S(1)}, f32[256]{0:T(256)}, u32[]{:S(2)}) copy-start(f32[256]{0:T(256)} %param.17) | copy-start | bytes 3076
where the time goes:
time: 152 us
  Pallas kernels  125 us (82%)
  other arithmetic  17.3 us (11%)
  local copies, waits for them, and re-layouts  8.55 us (6%)
  between operations  1.56 us (1%)
    pallas_call x1, Pallas kernels, body(): pl.pallas_call(functools.partial(columns_kernel, tile_count, epoch_count,...  69.6 us
    pallas_call x1, Pallas kernels, body(): pl.pallas_call(functools.partial(grid_kernel, pairs, tile_count, epoch_co...  31 us
    pallas_call x1, Pallas kernels, body(): pl.pallas_call(functools.partial(rows_kernel, pairs), out_shape=[jax.Shap...  15.2 us
    pallas_call x1, Pallas kernels, body(): pl.pallas_call(functools.partial(place_kernel, pairs), out_shape=jax.Shap...  8.84 us
    mul x1, other arithmetic, body(): image_sum * (image_scale * taper_rows)[:, :, None]  3.21 us
    reduce_sum x2, other arithmetic, places(): counts = jnp.sum(table[:, :, 0].reshape(-1, tile_count * capacity), 1)  3.19 us
    squeeze x1, local copies, waits for them, and re-layouts, body(): lax.dynamic_index_in_dim(jnp.asarray(last), epoch_index, 0, keepdims=False)  3.09 us

commit v1 on v0

v1 whole, which is shorter than its diff:
```python
import functools
import math

import jax
import jax.numpy as jnp
import numpy as np
from jax import lax
from jax.experimental import pallas as pl
from jax.experimental.pallas import tpu as pltpu
from jax.sharding import PartitionSpec as P

SUB = 32
LANES = 128
EDGE = 16
FIELDS = 8
UNROLL = 8
VMEM_BYTES = 56 * 1024 * 1024
MESH = pl.DeviceIdType.MESH


def dft(values, wanted, modulus=None):
    count = len(values)
    if all(v is None for v in values):
        return [None] * wanted
    if count == 1:
        return list(values)
    half = count // 2
    need = min(wanted, half)
    even, odd = dft(values[0::2], need), dft(values[1::2], need)
    low, high = [], []
    for k in range(need):
        e, o = even[k], odd[k]
        t = None if o is None else turn(o, k, count)
        low.append(plus(e, t))
        if half + k < wanted:
            high.append(minus(e, t))
    return low + high


def turn(value, k, count):
    re, im = value
    s = math.sqrt(0.5)
    k %= count
    if k == 0:
        return re, im
    if 2 * k == count:
        return -re, -im
    if 4 * k == count:
        return -im, re
    if 8 * k == count:
        return (re - im) * s, (re + im) * s
    if 8 * k == 3 * count:
        return (re + im) * -s, (re - im) * s
    c, s = math.cos(2 * math.pi * k / count), math.sin(2 * math.pi * k / count)
    return re * c - im * s, re * s + im * c


def plus(a, b):
    if a is None or b is None:
        return b if a is None else a
    return a[0] + b[0], a[1] + b[1]


def minus(a, b):
    if b is None:
        return a
    if a is None:
        return -b[0], -b[1]
    return a[0] - b[0], a[1] - b[1]


def epoch_turn(value, j, epoch, epoch_count):
    angles = [2 * math.pi * ((j * e) % epoch_count) / epoch_count for e in range(epoch_count)]

    def pick(numbers):
        chosen = jnp.float32(numbers[0])
        for e in range(1, epoch_count):
            chosen = jnp.where(epoch == e, jnp.float32(numbers[e]), chosen)
        return chosen

    cos, sin = [round(math.cos(a), 15) for a in angles], [round(math.sin(a), 15) for a in angles]
    re, im = value
    if not any(sin):
        if all(c == 1.0 for c in cos):
            return value
        c = pick(cos)
        return re * c, im * c
    c, s = pick(cos), pick(sin)
    return re * c - im * s, re * s + im * c


def grid_kernel(
    sizes, owner_ref, row_ref, col_ref, coords_ref, samples_ref, pool_ref, meta_ref, *scratch
):
    tile_count, epoch_count, capacity, lane_step, band = sizes
    packed, points, t_send, t_recv, x_send, x_recv = scratch
    me, epoch = lax.axis_index("tile"), lax.axis_index("epoch")
    n_slots = owner_ref.shape[1]
    n_samples = coords_ref.shape[1] // 2
    half = tile_count // 2
    per_meta = LANES // lane_step
    groups = -(-tile_count // per_meta)
    slot_rows = SUB // 2

    barrier = pltpu.get_barrier_semaphore()

    def greet(k, carry):
        peer = lax.rem(me + k, tile_count)
        pl.semaphore_signal(barrier, inc=1, device_id={"tile": peer}, device_id_type=MESH)
        return carry

    lax.fori_loop(1, tile_count, greet, 0)
    for k in range(1, epoch_count):
        peer = lax.rem(epoch + k, epoch_count)
        pl.semaphore_signal(barrier, inc=1, device_id={"epoch": peer}, device_id_type=MESH)

    owner = owner_ref[...]
    mirrored = owner >= half
    target = jnp.where(mirrored, 2 * (tile_count - 1 - owner) + 1, 2 * owner)
    row = jnp.where(mirrored, band - (SUB - 1) - row_ref[...], row_ref[...])
    col = jnp.where(mirrored, tile_count * band - (SUB - 1) - col_ref[...], col_ref[...])
    mine = lax.broadcasted_iota(jnp.int32, (tile_count, n_slots), 0) == target
    before = lax.broadcasted_iota(jnp.int32, (n_slots, n_slots), 0) < lax.broadcasted_iota(
        jnp.int32, (n_slots, n_slots), 1
    )
    rank = jnp.dot(
        jnp.where(mine, 1.0, 0.0).astype(jnp.bfloat16),
        jnp.where(before, 1.0, 0.0).astype(jnp.bfloat16),
        preferred_element_type=jnp.float32,
    ).astype(jnp.int32)
    key = jnp.where(mine, rank, -LANES)
    fields = [jnp.ones_like(row), row, col // LANES, col % LANES]
    fields = jnp.concatenate(fields + [jnp.zeros_like(row)] * (EDGE - len(fields)), 0)
    fields = fields.astype(jnp.float32).astype(jnp.bfloat16)
    lane = lax.broadcasted_iota(jnp.int32, (LANES, n_slots), 0) - lax.rem(me, per_meta) * lane_step
    first = lax.broadcasted_iota(jnp.int32, (lane_step, n_slots), 0)
    hits = []
    for t in range(tile_count):
        hits.append(jnp.where(key[t : t + 1] == first, 1.0, 0.0))
        spot = jnp.where(key[t : t + 1] == lane, 1.0, 0.0).astype(jnp.bfloat16)
        packed[t, capacity * slot_rows :, :] = lax.dot_general(
            fields, spot, (((1,), (1,)), ((), ())), preferred_element_type=jnp.float32
        ).astype(jnp.bfloat16)
    hits = jnp.concatenate(hits, 0)
    here = jnp.dot(
        hits,
        coords_ref[...] * 0.25,
        precision=lax.Precision.HIGHEST,
        preferred_element_type=jnp.float32,
    )
    values = jnp.dot(
        hits.astype(jnp.bfloat16), samples_ref[...], preferred_element_type=jnp.float32
    )
    for t in range(tile_count):
        rows = slice(t * lane_step, (t + 1) * lane_step)
        points[t, 0:lane_step] = here[rows]
        points[t, lane_step:] = values[rows]

    pl.semaphore_wait(barrier, tile_count + epoch_count - 2)

    cell_iota = lax.broadcasted_iota(jnp.int32, (SUB, n_samples), 0)

    def weights(cells, at):
        distance = cells - at
        return jnp.square(jnp.maximum(1.0 - distance * distance, 0.0))

    def make(tile):
        flip = lax.rem(tile, 2)
        cells = jnp.where(flip == 1, SUB - 1 - cell_iota, cell_iota).astype(jnp.float32) * 0.25
        sign = (1 - 2 * flip).astype(jnp.float32)
        for k in range(capacity):
            along_u = weights(cells, points[tile, k : k + 1, :n_samples]).astype(jnp.bfloat16)
            along_v = weights(cells, points[tile, k : k + 1, n_samples:])
            at = lane_step + k
            re = points[tile, at : at + 1, :n_samples] * along_v
            im = (points[tile, at : at + 1, n_samples:] * sign) * along_v
            subgrid = lax.dot_general(
                along_u,
                jnp.concatenate([re, im], 0).astype(jnp.bfloat16),
                (((1,), (1,)), ((), ())),
                preferred_element_type=jnp.float32,
            )
            packed[tile, k * slot_rows : (k + 1) * slot_rows, :] = jnp.concatenate(
                [subgrid[:slot_rows], subgrid[slot_rows:]], 1
            ).astype(jnp.bfloat16)

    def tile_copy(k):
        peer = lax.rem(me + k, tile_count)
        return pltpu.make_async_remote_copy(
            src_ref=packed.at[peer],
            dst_ref=pool_ref.at[me],
            send_sem=t_send.at[k],
            recv_sem=t_recv.at[k],
            device_id={"tile": peer},
            device_id_type=MESH,
        )

    def epoch_copy(k, j):
        origin = lax.rem(me + tile_count - k, tile_count)
        return pltpu.make_async_remote_copy(
            src_ref=pool_ref.at[origin],
            dst_ref=pool_ref.at[j * tile_count + origin],
            send_sem=x_send.at[(j - 1) * tile_count + k],
            recv_sem=x_recv.at[(j - 1) * tile_count + k],
            device_id={"epoch": lax.rem(epoch + j, epoch_count)},
            device_id_type=MESH,
        )

    make(me)
    pool_ref[me] = packed[me]
    for j in range(1, epoch_count):
        epoch_copy(0, j).start()

    def send(k, carry):
        make(lax.rem(me + k, tile_count))
        tile_copy(k).start()
        return carry

    lax.fori_loop(1, tile_count, send, 0)

    def forward(k, carry):
        tile_copy(k).wait_recv()
        for j in range(1, epoch_count):
            epoch_copy(k, j).start()
        return carry

    lax.fori_loop(1, tile_count, forward, 0)

    def sent_all(k, carry):
        tile_copy(k).wait_send()
        return carry

    lax.fori_loop(1, tile_count, sent_all, 0)

    def crossed(k, carry):
        for j in range(1, epoch_count):
            epoch_copy(k, j).wait()
        return carry

    lax.fori_loop(0, tile_count, crossed, 0)

    for j in range(epoch_count):
        for g in range(groups):
            total = jnp.zeros((EDGE, LANES), jnp.float32)
            for s in range(g * per_meta, min(tile_count, (g + 1) * per_meta)):
                total += pool_ref[j * tile_count + s, capacity * slot_rows :, :].astype(jnp.float32)
            meta_ref[j * groups + g] = total[:FIELDS].astype(jnp.int32)


def band_kernel(
    sizes, meta_ref, pool_ref, cos_ref, sin_ref, second_ref, out_ref, acc, turned_ref, wanted, scale
):
    tile_count, epoch_count, capacity, lane_step, band = sizes
    epoch = lax.axis_index("epoch")
    lane_blocks, acc_rows = acc.shape[1] - 1, acc.shape[2]
    rows_here = band // epoch_count
    spare = acc_rows - SUB
    slot_rows = SUB // 2
    per_meta = LANES // lane_step
    groups = -(-tile_count // per_meta)
    first_row = epoch * rows_here - SUB

    def clear(i, carry):
        acc[0, i] = jnp.zeros((acc_rows, LANES), jnp.float32)
        acc[1, i] = jnp.zeros((acc_rows, LANES), jnp.float32)
        return carry

    lax.fori_loop(0, lane_blocks + 1, clear, 0)

    found = jnp.int32(0)
    for e in range(epoch_count):
        held = jnp.int32(0)
        for g in range(groups):
            at = e * groups + g

            def look(s, carry, at=at):
                found, held = carry
                for k in range(capacity):
                    lane = s * lane_step + k
                    valid = meta_ref[at, 0, lane]
                    row = meta_ref[at, 1, lane] - first_row
                    inside = (valid > 0) & (row > 0) & (row < rows_here + SUB)
                    wanted[found] = at * LANES + lane
                    found += jnp.where(inside, 1, 0)
                    held += valid
                return found, held

            count = min(tile_count - g * per_meta, per_meta)
            found, held = lax.fori_loop(0, count, look, (found, held))
        scale[e] = 1.0 / jnp.full((SUB, LANES), jnp.maximum(held, 1), jnp.int32).astype(jnp.float32)
    for k in range(UNROLL):
        wanted[found + k] = -1

    shape = (SUB, 2 * LANES)
    steps = lax.broadcasted_iota(jnp.int32, shape, 1) - lax.broadcasted_iota(jnp.int32, shape, 0)

    def per_batch(b, carry):
        placed = []
        for k in range(UNROLL):
            entry = wanted[b * UNROLL + k]
            index = jnp.maximum(entry, 0)
            at, lane = index // LANES, lax.rem(index, LANES)
            e, g = at // groups, lax.rem(at, groups)
            source = e * tile_count + g * per_meta + lane // lane_step
            row = jnp.where(entry < 0, spare, meta_ref[at, 1, lane] - first_row)
            block = meta_ref[at, 2, lane]
            start = meta_ref[at, 3, lane]
            first = pl.multiple_of(lax.rem(lane, lane_step) * slot_rows, slot_rows)
            data = pool_ref[source, pl.ds(first, slot_rows), :]
            parts = jnp.concatenate(
                [data[:, i * SUB : (i + 1) * SUB] for i in (0, 2, 1, 3)], 0
            )
            select = jnp.where(steps == start, 1.0, 0.0).astype(jnp.bfloat16)
            window = jnp.dot(parts, select, preferred_element_type=jnp.float32)
            placed.append((row, block, scale[e], window))
        for row, block, factor, window in placed:
            for p in range(2):
                for h in range(2):
                    acc[p, block + h, pl.ds(row, SUB), :] += (
                        window[p * SUB : (p + 1) * SUB, h * LANES : (h + 1) * LANES] * factor
                    )
        return carry

    lax.fori_loop(0, (found + UNROLL - 1) // UNROLL, per_batch, 0)

    block_len = band
    group = min(16, rows_here)
    width = min(LANES, block_len)
    chunks = block_len // width

    def per_group(first, size):
        for h in range(chunks):
            values = []
            for a in range(tile_count):
                col = a * block_len + h * width
                lane, at = col % LANES, col // LANES
                value = [acc[p, at, pl.ds(SUB + first, size), lane : lane + width] for p in range(2)]
                if col == 0:
                    for p in range(2):
                        value[p] += acc[p, lane_blocks, pl.ds(SUB + first, size), :width]
                values.append(tuple(value))
            lanes = slice(h * width, (h + 1) * width)
            for m, (re, im) in enumerate(dft(values, tile_count)):
                c, s = cos_ref[m : m + 1, lanes], sin_ref[m : m + 1, lanes]
                turned = (re * c - im * s, re * s + im * c)
                for p in range(2):
                    start = p * block_len + h * width
                    turned_ref[m, pl.ds(first, size), start : start + width] = turned[p].astype(
                        jnp.bfloat16
                    )

    def row_group(i, carry):
        per_group(pl.multiple_of(i * group, group), group)
        return carry

    lax.fori_loop(0, rows_here // group, row_group, 0)
    per_group(rows_here, EDGE)

    parts = 2 * chunks
    edge_row = lax.broadcasted_iota(jnp.int32, (EDGE, width), 0)
    has_edge = jnp.where(epoch == epoch_count - 1, 1.0, 0.0)

    def per_tile(m, carry):
        moved = jnp.dot(turned_ref[m], second_ref[...], preferred_element_type=jnp.float32)
        edge = jnp.zeros((EDGE, width), jnp.float32)
        for q in range(parts):
            piece = moved[:, q * width : (q + 1) * width]
            out_ref[m, q * rows_here : (q + 1) * rows_here, :] = piece[:rows_here].astype(
                jnp.bfloat16
            )
            edge = jnp.where(edge_row == q, piece[rows_here : rows_here + 1] * has_edge, edge)
        out_ref[m, parts * rows_here :, :] = edge.astype(jnp.bfloat16)
        return carry

    lax.fori_loop(0, tile_count, per_tile, 0)


def swap_kernel(tile_count, epoch_count, own_ref, full_ref, *scratch):
    landed, folded, p_send, p_recv, t_send, t_recv, x_send, x_recv = scratch
    me, epoch = lax.axis_index("tile"), lax.axis_index("epoch")
    half = tile_count // 2
    mine, side = me // 2, lax.rem(me, 2)
    partner = me + 1 - 2 * side

    barrier = pltpu.get_barrier_semaphore()

    def greet(k, carry):
        peer = lax.rem(mine + k, half) * 2 + side
        pl.semaphore_signal(barrier, inc=1, device_id={"tile": peer}, device_id_type=MESH)
        return carry

    lax.fori_loop(1, half, greet, 0)
    pl.semaphore_signal(barrier, inc=1, device_id={"tile": partner}, device_id_type=MESH)
    for k in range(1, epoch_count):
        peer = lax.rem(epoch + k, epoch_count)
        pl.semaphore_signal(barrier, inc=1, device_id={"epoch": peer}, device_id_type=MESH)
    pl.semaphore_wait(barrier, half + epoch_count - 1)

    def partner_copy(k):
        return pltpu.make_async_remote_copy(
            src_ref=own_ref.at[lax.rem(mine + k, half) * 2 + 1 - side],
            dst_ref=landed.at[k],
            send_sem=p_send.at[k],
            recv_sem=p_recv.at[k],
            device_id={"tile": partner},
            device_id_type=MESH,
        )

    def tile_copy(k):
        return pltpu.make_async_remote_copy(
            src_ref=folded.at[k],
            dst_ref=full_ref.at[epoch * half + mine],
            send_sem=t_send.at[k],
            recv_sem=t_recv.at[k],
            device_id={"tile": lax.rem(mine + k, half) * 2 + side},
            device_id_type=MESH,
        )

    def epoch_copy(k, j):
        origin = epoch * half + lax.rem(mine + half - k, half)
        return pltpu.make_async_remote_copy(
            src_ref=full_ref.at[origin],
            dst_ref=full_ref.at[origin],
            send_sem=x_send.at[(j - 1) * half + k],
            recv_sem=x_recv.at[(j - 1) * half + k],
            device_id={"epoch": lax.rem(epoch + j, epoch_count)},
            device_id_type=MESH,
        )

    def give(k, carry):
        partner_copy(k).start()
        return carry

    lax.fori_loop(0, half, give, 0)

    def fold(k):
        partner_copy(k).wait_recv()
        both = own_ref[lax.rem(mine + k, half) * 2 + side].astype(jnp.float32) + landed[k].astype(
            jnp.float32
        )
        return both.astype(jnp.bfloat16)

    full_ref[epoch * half + mine] = fold(0)
    for j in range(1, epoch_count):
        epoch_copy(0, j).start()

    def send(k, carry):
        folded[k] = fold(k)
        tile_copy(k).start()
        return carry

    lax.fori_loop(1, half, send, 0)

    def forward(k, carry):
        tile_copy(k).wait_recv()
        for j in range(1, epoch_count):
            epoch_copy(k, j).start()
        return carry

    lax.fori_loop(1, half, forward, 0)

    def finish(k, carry):
        tile_copy(k).wait_send()
        return carry

    lax.fori_loop(1, half, finish, 0)

    def settle(k, carry):
        partner_copy(k).wait_send()
        for j in range(1, epoch_count):
            epoch_copy(k, j).wait()
        return carry

    lax.fori_loop(0, half, settle, 0)


def image_kernel(
    sizes, image_scale, epoch_ref, full_ref, last_ref, rows_ref, cols_ref, out_ref, mixed
):
    tile_count, epoch_count = sizes
    half, kept = tile_count // 2, tile_count // epoch_count
    width = full_ref.shape[2]
    block_len = out_ref.shape[1]
    chunks = block_len // width
    parts = 2 * chunks
    rows_here = block_len // epoch_count
    group = min(16, rows_here)
    epoch = epoch_ref[0]

    @pl.when(pl.program_id(0) == 0)
    def _():
        def per_group(e, first, edges):
            for h in range(chunks):
                values = []
                for j in range(half):
                    value = tuple(
                        full_ref[
                            e * half + j, pl.ds((h * 2 + p) * rows_here + first, group), :
                        ].astype(jnp.float32)
                        for p in range(2)
                    )
                    values.append(epoch_turn(value, j, epoch, epoch_count))
                done = dft(values + [None] * half, kept)
                if edges is not None:
                    top = lax.broadcasted_iota(jnp.int32, (group, width), 0) == 0
                    done = [
                        tuple(a + jnp.where(top, b, 0.0) for a, b in zip(part, edge))
                        for part, edge in zip(done, edges[h])
                    ]
                for c, part in enumerate(done):
                    for p in range(2):
                        row = p * block_len + e * rows_here + first
                        if not isinstance(row, int):
                            row = pl.multiple_of(row, group)
                        mixed[c, pl.ds(row, group), h * width : (h + 1) * width] = part[p].astype(
                            jnp.bfloat16
                        )

        edges = []
        for h in range(chunks):
            values = [None]
            for j in range(half):
                block = full_ref[(epoch_count - 1) * half + j, parts * rows_here :, :].astype(
                    jnp.float32
                )
                value = tuple(block[h * 2 + p : h * 2 + p + 1] for p in range(2))
                values.append(epoch_turn(value, j + 1, epoch, epoch_count))
            edges.append(dft(values + [None] * (tile_count - half - 1), kept))
        per_group(0, 0, edges)
        for e in range(epoch_count):

            def step(i, carry, e=e):
                per_group(e, pl.multiple_of(i * group, group), None)
                return carry

            lax.fori_loop(1 if e == 0 else 0, rows_here // group, step, 0)

    c = pl.program_id(0)
    pixels = jnp.dot(last_ref[0], mixed[c], preferred_element_type=jnp.float32)
    out_ref[0] = pixels * (rows_ref[0] * image_scale) * cols_ref[...]


def turns(product, modulus):
    angles = (product % modulus) * (2.0 * math.pi / modulus)
    return np.cos(angles), np.sin(angles)


def make_tables(tile_count, block_len):
    grid_size = tile_count * block_len
    long_idx = np.arange(block_len)
    tile_idx = np.arange(tile_count)
    turn_cos, turn_sin = turns(tile_idx[:, None] * long_idx[None, :], grid_size)
    c, s = turns(long_idx[:, None] * long_idx[None, :], block_len)
    second = np.stack([np.stack([c, s], 1), np.stack([-s, c], 1)], 0)
    width = min(LANES, block_len)
    second = second.reshape(2 * block_len, 2, block_len // width, width)
    second = second.transpose(0, 2, 1, 3).reshape(2 * block_len, 2 * block_len)
    pixel = long_idx[None, :] * tile_count + tile_idx[:, None]
    c, s = turns(pixel[:, :, None] * long_idx[None, None, :], grid_size)
    last = np.concatenate([c, -s], -1)
    return (
        turn_cos.astype(np.float32),
        turn_sin.astype(np.float32),
        second.astype(jnp.bfloat16),
        last.astype(jnp.bfloat16),
    )


def vmem(count):
    return [pl.BlockSpec(memory_space=pltpu.VMEM)] * count


def body(tables, owners, row_offsets, col_offsets, samples, coords, taper_rows, taper_cols):
    tile_count = lax.axis_size("tile")
    epoch_count = lax.axis_size("epoch")
    n_slots = owners.shape[1]
    n_samples = samples.shape[3]
    capacity = max(2, n_slots * 5 // (4 * tile_count))
    capacity += capacity % 2
    lane_step = max(8, 1 << (capacity - 1).bit_length())
    band = taper_cols.shape[0]
    width = min(LANES, band)
    half, kept = tile_count // 2, tile_count // epoch_count
    rows_here = band // epoch_count
    parts = 2 * (band // width)
    turn_cos, turn_sin, second, last = tables
    sizes = (tile_count, epoch_count, capacity, lane_step, band)
    block_rows = capacity * SUB // 2 + EDGE
    meta_rows = epoch_count * -(-tile_count // (LANES // lane_step))

    tile_sems = pltpu.SemaphoreType.DMA((tile_count,))
    epoch_sems = pltpu.SemaphoreType.DMA(((epoch_count - 1) * tile_count,))
    pool, meta = pl.pallas_call(
        functools.partial(grid_kernel, sizes),
        out_shape=[
            jax.ShapeDtypeStruct((epoch_count * tile_count, block_rows, LANES), jnp.bfloat16),
            jax.ShapeDtypeStruct((meta_rows, FIELDS, LANES), jnp.int32),
        ],
        in_specs=vmem(5),
        out_specs=vmem(2),
        scratch_shapes=[
            pltpu.VMEM((tile_count, block_rows, LANES), jnp.bfloat16),
            pltpu.VMEM((tile_count, 2 * lane_step, 2 * n_samples), jnp.float32),
            tile_sems,
            tile_sems,
            epoch_sems,
            epoch_sems,
        ],
        compiler_params=pltpu.CompilerParams(
            vmem_limit_bytes=VMEM_BYTES, collective_id=1, has_side_effects=True
        ),
        name="grid_slots",
    )(
        owners,
        row_offsets,
        col_offsets,
        coords.reshape(n_slots, 2 * n_samples),
        samples.reshape(n_slots, 2 * n_samples),
    )

    lane_blocks = tile_count * band // LANES
    block_shape = (parts * rows_here + EDGE, width)
    own = pl.pallas_call(
        functools.partial(band_kernel, sizes),
        out_shape=jax.ShapeDtypeStruct((tile_count, *block_shape), jnp.bfloat16),
        in_specs=[pl.BlockSpec(memory_space=pltpu.SMEM)] + vmem(4),
        out_specs=vmem(1)[0],
        scratch_shapes=[
            pltpu.VMEM((2, lane_blocks + 1, rows_here + 3 * SUB, LANES), jnp.float32),
            pltpu.VMEM((tile_count, rows_here + EDGE, 2 * band), jnp.bfloat16),
            pltpu.SMEM((epoch_count * tile_count * capacity + UNROLL,), jnp.int32),
            pltpu.VMEM((epoch_count, SUB, LANES), jnp.float32),
        ],
        compiler_params=pltpu.CompilerParams(vmem_limit_bytes=VMEM_BYTES),
        name="band_rows",
    )(meta, pool, jnp.asarray(turn_cos), jnp.asarray(turn_sin), jnp.asarray(second))

    half_sems = pltpu.SemaphoreType.DMA((half,))
    epoch_sems = pltpu.SemaphoreType.DMA(((epoch_count - 1) * half,))
    full = pl.pallas_call(
        functools.partial(swap_kernel, tile_count, epoch_count),
        out_shape=jax.ShapeDtypeStruct((epoch_count * half, *block_shape), jnp.bfloat16),
        in_specs=vmem(1),
        out_specs=vmem(1)[0],
        scratch_shapes=[
            pltpu.VMEM((half, *block_shape), jnp.bfloat16),
            pltpu.VMEM((half, *block_shape), jnp.bfloat16),
            half_sems,
            half_sems,
            half_sems,
            half_sems,
            epoch_sems,
            epoch_sems,
        ],
        compiler_params=pltpu.CompilerParams(
            vmem_limit_bytes=VMEM_BYTES, collective_id=0, has_side_effects=True
        ),
        name="swap_rows",
    )(own)

    image_scale = math.sqrt(n_slots) / (64.0 * tile_count * math.sqrt(epoch_count))
    return pl.pallas_call(
        functools.partial(image_kernel, (tile_count, epoch_count), image_scale),
        grid_spec=pltpu.PrefetchScalarGridSpec(
            num_scalar_prefetch=1,
            grid=(kept,),
            in_specs=[
                pl.BlockSpec(memory_space=pltpu.VMEM),
                pl.BlockSpec((1, band, 2 * band), lambda c, e: (e[0] * kept + c, 0, 0)),
                pl.BlockSpec((1, band, 1), lambda c, e: (c, 0, 0)),
                pl.BlockSpec((1, band), lambda c, e: (0, 0)),
            ],
            out_specs=pl.BlockSpec((1, band, band), lambda c, e: (c, 0, 0)),
            scratch_shapes=[pltpu.VMEM((kept, 2 * band, band), jnp.bfloat16)],
        ),
        out_shape=jax.ShapeDtypeStruct((kept, band, band), jnp.float32),
        compiler_params=pltpu.CompilerParams(vmem_limit_bytes=VMEM_BYTES),
        name="image_rows",
    )(
        lax.axis_index("epoch").astype(jnp.int32)[None],
        full,
        jnp.asarray(last),
        taper_rows[:, :, None],
        taper_cols[None, :],
    )


def solution(mesh):
    placed = (
        P("epoch", "tile"),
        P("epoch", "tile"),
        P("epoch", "tile"),
        P("epoch", "tile", None, None),
        P("epoch", "tile", None, None),
        P("epoch", None),
        P("tile"),
    )

    def whole(owners, row_offsets, col_offsets, samples, coords, taper_rows, taper_cols):
        tables = make_tables(mesh.shape["tile"], taper_cols.shape[0] // mesh.shape["tile"])
        return jax.shard_map(
            functools.partial(body, tables),
            mesh=mesh,
            in_specs=placed,
            out_specs=P("epoch", None, "tile"),
            check_vma=False,
        )(owners, row_offsets, col_offsets, samples, coords, taper_rows, taper_cols)

    return whole
```

time: 152 us -> 111 us (0.73)
  the two profiles are of different devices: /device:TPU:31 before, /device:TPU:27 now
where the time goes in v1:
time: 111 us; the launch traced here: 110 us
  Pallas kernels  106 us (95%)
  local copies, waits for them, and re-layouts  4.58 us (4%)
    pallas_call x1, Pallas kernels, body(): pl.pallas_call(functools.partial(swap_kernel, tile_count, epoch_count), o...  48.7 us
    pallas_call x1, Pallas kernels, body(): pl.pallas_call(functools.partial(grid_kernel, sizes), out_shape=[jax.Shap...  32.8 us
    pallas_call x1, Pallas kernels, body(): pl.pallas_call(functools.partial(band_kernel, sizes), out_shape=jax.Shape...  15.1 us
    pallas_call x1, Pallas kernels, body(): pl.pallas_call(functools.partial(image_kernel, (tile_count, epoch_count),...  9.1 us
    unnamed x4, local copies, waits for them, and re-layouts  3.22 us

profile of v1, /device:TPU:27, one launch (start us, length us, event | category | flops | bytes accessed | tf_op | source)
XLA Modules:
  0.0 110.3 jit_solution(14081515326873272882)
XLA Ops:
  0.0 1.7 %copy.13 = f32[16,8,2,256]{3,1,2,0:T(8,128)} copy(f32[16,8,2,256]{3,2,1,0:T(2,128)} %bitcast.11) | data formatting | bytes 524288
  1.7 1.6 %copy.14 = bf16[16,8,2,256]{3,1,2,0:T(8,128)(2,1)} copy(bf16[16,8,2,256]{3,2,1,0:T(2,128)(2,1)} %bitcast.12) | data formatting | bytes 262144
  3.2 32.8 %grid_slots.1 = (bf16[32,176,128]{2,1,0:T(8,128)(2,1)}, s32[4,8,128]{2,1,0:T(8,128)}) custom-call(s32[1,128]{1,0:T(1,128)} %owner_ref.1, s32[1,128]{1,0:T(1,128)} %row_ref.1, s32[1,128]{1,0:T(1,128)} %col_ref.1, f32[128,512]{1,0:T(8,128)} %bitcast.9, bf16[128,512]{1,0:T(8,128)(2,1)} %bitcast.10), custom_call_target="tpu_custom_call" | custom-call | tf_op jit(solution)/shard_map/grid_slots/pallas_call | solution.py:593
  36.1 15.1 %band_rows.1.own_ref = bf16[16,528,128]{2,1,0:T(8,128)(2,1)} custom-call(s32[4,8,128]{2,1,0:T(8,128)} %get-tuple-element.7.meta_ref, bf16[32,176,128]{2,1,0:T(8,128)(2,1)} %get-tuple-element.8.pool_ref, f32[16,256]{1,0:T(8,128)} %constant.14.clone.cos_ref, f32[16,256]{1,0:T(8,128)} %constant.15.clone.sin_ref, bf16[512,512]{1,0:T(8,128)(2,1)} %constant.16.clone.second_ref), custom_call_target="tpu_custom_call" | custom-call | tf_op jit(solution)/shard_map/band_rows/pallas_call | solution.py:623
  51.2 0.0 copy-start
  51.2 48.7 %swap_rows.1.full_ref = bf16[16,528,128]{2,1,0:T(8,128)(2,1)} custom-call(bf16[16,528,128]{2,1,0:T(8,128)(2,1)} %band_rows.1.own_ref), custom_call_target="tpu_custom_call" | custom-call | tf_op jit(solution)/shard_map/swap_rows/pallas_call | solution.py:640
  99.9 0.0 copy-done
  99.9 1.4 %copy.12.rows_ref = f32[8,256,1]{2,1,0:T(8,128)} copy(f32[8,256,1]{1,0,2:T(8,128)S(1)} %bitcast.13) | data formatting | bytes 16384 | tf_op jit(solution)/shard_map/broadcast_in_dim | solution.py:683
  101.2 9.1 %image_rows.1 = f32[8,256,256]{2,1,0:T(8,128)} custom-call(s32[1]{0:T(128)} %bitcast.epoch_ref, bf16[16,528,128]{2,1,0:T(8,128)(2,1)} %swap_rows.1.full_ref, bf16[16,256,512]{2,1,0:T(8,128)(2,1)} %constant.17.clone.last_ref, f32[8,256,1]{2,1,0:T(8,128)} %copy.12.rows_ref, f32[1,256]{1,0:T(1,128)} %bitcast.14), custom_call_target="tpu_custom_call" | custom-call | tf_op jit(solution)/shard_map/image_rows/pallas_call | solution.py:662
Async XLA Ops:
  51.2 48.7 %copy-start = (f32[8,256]{1,0:T(8,128)S(1)}, f32[8,256]{1,0:T(8,128)}, u32[]{:S(2)}) copy-start(f32[8,256]{1,0:T(8,128)} %param.16) | copy-start | bytes 24580

commit v2 on v1

--- a/solution.py
+++ b/solution.py
@@ -96,7 +96,7 @@
     packed, points, t_send, t_recv, x_send, x_recv = scratch
     me, epoch = lax.axis_index("tile"), lax.axis_index("epoch")
     n_slots = owner_ref.shape[1]
-    n_samples = coords_ref.shape[1] // 2
+    n_samples = coords_ref.shape[3]
     half = tile_count // 2
     per_meta = LANES // lane_step
     groups = -(-tile_count // per_meta)
@@ -144,13 +144,13 @@
     hits = jnp.concatenate(hits, 0)
     here = jnp.dot(
         hits,
-        coords_ref[...] * 0.25,
+        jnp.concatenate([coords_ref[0, :, p, :] for p in range(2)], 1) * 0.25,
         precision=lax.Precision.HIGHEST,
         preferred_element_type=jnp.float32,
     )
-    values = jnp.dot(
-        hits.astype(jnp.bfloat16), samples_ref[...], preferred_element_type=jnp.float32
-    )
+    samples = samples_ref[0].astype(jnp.float32)
+    samples = jnp.concatenate([samples[:, p, :] for p in range(2)], 1).astype(jnp.bfloat16)
+    values = jnp.dot(hits.astype(jnp.bfloat16), samples, preferred_element_type=jnp.float32)
     for t in range(tile_count):
         rows = slice(t * lane_step, (t + 1) * lane_step)
         points[t, 0:lane_step] = here[rows]
@@ -247,9 +247,7 @@
             meta_ref[j * groups + g] = total[:FIELDS].astype(jnp.int32)
 
 
-def band_kernel(
-    sizes, meta_ref, pool_ref, cos_ref, sin_ref, second_ref, out_ref, acc, turned_ref, wanted, scale
-):
+def place_kernel(sizes, meta_ref, pool_ref, acc, wanted, scale):
     tile_count, epoch_count, capacity, lane_step, band = sizes
     epoch = lax.axis_index("epoch")
     lane_blocks, acc_rows = acc.shape[1] - 1, acc.shape[2]
@@ -323,64 +321,23 @@
 
     lax.fori_loop(0, (found + UNROLL - 1) // UNROLL, per_batch, 0)
 
-    block_len = band
-    group = min(16, rows_here)
-    width = min(LANES, block_len)
-    chunks = block_len // width
-
-    def per_group(first, size):
-        for h in range(chunks):
-            values = []
-            for a in range(tile_count):
-                col = a * block_len + h * width
-                lane, at = col % LANES, col // LANES
-                value = [acc[p, at, pl.ds(SUB + first, size), lane : lane + width] for p in range(2)]
-                if col == 0:
-                    for p in range(2):
-                        value[p] += acc[p, lane_blocks, pl.ds(SUB + first, size), :width]
-                values.append(tuple(value))
-            lanes = slice(h * width, (h + 1) * width)
-            for m, (re, im) in enumerate(dft(values, tile_count)):
-                c, s = cos_ref[m : m + 1, lanes], sin_ref[m : m + 1, lanes]
-                turned = (re * c - im * s, re * s + im * c)
-                for p in range(2):
-                    start = p * block_len + h * width
-                    turned_ref[m, pl.ds(first, size), start : start + width] = turned[p].astype(
-                        jnp.bfloat16
-                    )
-
-    def row_group(i, carry):
-        per_group(pl.multiple_of(i * group, group), group)
-        return carry
-
-    lax.fori_loop(0, rows_here // group, row_group, 0)
-    per_group(rows_here, EDGE)
-
-    parts = 2 * chunks
-    edge_row = lax.broadcasted_iota(jnp.int32, (EDGE, width), 0)
-    has_edge = jnp.where(epoch == epoch_count - 1, 1.0, 0.0)
-
-    def per_tile(m, carry):
-        moved = jnp.dot(turned_ref[m], second_ref[...], preferred_element_type=jnp.float32)
-        edge = jnp.zeros((EDGE, width), jnp.float32)
-        for q in range(parts):
-            piece = moved[:, q * width : (q + 1) * width]
-            out_ref[m, q * rows_here : (q + 1) * rows_here, :] = piece[:rows_here].astype(
-                jnp.bfloat16
-            )
-            edge = jnp.where(edge_row == q, piece[rows_here : rows_here + 1] * has_edge, edge)
-        out_ref[m, parts * rows_here :, :] = edge.astype(jnp.bfloat16)
-        return carry
-
-    lax.fori_loop(0, tile_count, per_tile, 0)
-
-
-def swap_kernel(tile_count, epoch_count, own_ref, full_ref, *scratch):
-    landed, folded, p_send, p_recv, t_send, t_recv, x_send, x_recv = scratch
+
+def swap_kernel(sizes, cuts, acc_ref, cos_ref, sin_ref, second_ref, mixed_ref, *scratch):
+    tile_count, epoch_count, band = sizes
+    turned, given, landed, folded, full = scratch[:5]
+    p_send, p_recv, t_send, t_recv, x_send, x_recv = scratch[5:]
     me, epoch = lax.axis_index("tile"), lax.axis_index("epoch")
-    half = tile_count // 2
+    half, kept = tile_count // 2, tile_count // epoch_count
     mine, side = me // 2, lax.rem(me, 2)
     partner = me + 1 - 2 * side
+    rows_here = band // epoch_count
+    cut_rows = rows_here // cuts
+    width = min(LANES, band)
+    chunks = band // width
+    parts = 2 * chunks
+    lane_blocks = acc_ref.shape[1] - 1
+    group = min(16, cut_rows)
+    batch = min(4, half)
 
     barrier = pltpu.get_barrier_semaphore()
 
@@ -394,150 +351,218 @@
     for k in range(1, epoch_count):
         peer = lax.rem(epoch + k, epoch_count)
         pl.semaphore_signal(barrier, inc=1, device_id={"epoch": peer}, device_id_type=MESH)
-    pl.semaphore_wait(barrier, half + epoch_count - 1)
-
-    def partner_copy(k):
+
+    def rows_of(cut):
+        edge = EDGE if cut == cuts - 1 else 0
+        return pl.ds(cut * parts * cut_rows, parts * cut_rows + edge)
+
+    def partner_copy(cut, k):
         return pltpu.make_async_remote_copy(
-            src_ref=own_ref.at[lax.rem(mine + k, half) * 2 + 1 - side],
-            dst_ref=landed.at[k],
-            send_sem=p_send.at[k],
-            recv_sem=p_recv.at[k],
+            src_ref=given.at[k, rows_of(cut)],
+            dst_ref=landed.at[k, rows_of(cut)],
+            send_sem=p_send.at[cut * half + k],
+            recv_sem=p_recv.at[cut * half + k],
             device_id={"tile": partner},
             device_id_type=MESH,
         )
 
-    def tile_copy(k):
+    def tile_copy(cut, k):
         return pltpu.make_async_remote_copy(
-            src_ref=folded.at[k],
-            dst_ref=full_ref.at[epoch * half + mine],
-            send_sem=t_send.at[k],
-            recv_sem=t_recv.at[k],
+            src_ref=folded.at[k, rows_of(cut)],
+            dst_ref=full.at[epoch * half + mine, rows_of(cut)],
+            send_sem=t_send.at[cut * half + k],
+            recv_sem=t_recv.at[cut * half + k],
             device_id={"tile": lax.rem(mine + k, half) * 2 + side},
             device_id_type=MESH,
         )
 
-    def epoch_copy(k, j):
+    def epoch_copy(cut, k, j):
         origin = epoch * half + lax.rem(mine + half - k, half)
+        at = (cut * (epoch_count - 1) + j - 1) * half + k
         return pltpu.make_async_remote_copy(
-            src_ref=full_ref.at[origin],
-            dst_ref=full_ref.at[origin],
-            send_sem=x_send.at[(j - 1) * half + k],
-            recv_sem=x_recv.at[(j - 1) * half + k],
+            src_ref=full.at[origin, rows_of(cut)],
+            dst_ref=full.at[origin, rows_of(cut)],
+            send_sem=x_send.at[at],
+            recv_sem=x_recv.at[at],
             device_id={"epoch": lax.rem(epoch + j, epoch_count)},
             device_id_type=MESH,
         )
 
-    def give(k, carry):
-        partner_copy(k).start()
-        return carry
-
-    lax.fori_loop(0, half, give, 0)
-
-    def fold(k):
-        partner_copy(k).wait_recv()
-        both = own_ref[lax.rem(mine + k, half) * 2 + side].astype(jnp.float32) + landed[k].astype(
-            jnp.float32
+    def transform(first, size):
+        for h in range(chunks):
+            values = []
+            for a in range(tile_count):
+                col = a * band + h * width
+                lane, at = col % LANES, col // LANES
+                value = [
+                    acc_ref[p, at, pl.ds(SUB + first, size), lane : lane + width] for p in range(2)
+                ]
+                if col == 0:
+                    for p in range(2):
+                        value[p] += acc_ref[p, lane_blocks, pl.ds(SUB + first, size), :width]
+                values.append(tuple(value))
+            lanes = slice(h * width, (h + 1) * width)
+            for m, (re, im) in enumerate(dft(values, tile_count)):
+                c, s = cos_ref[m : m + 1, lanes], sin_ref[m : m + 1, lanes]
+                pair = (re * c - im * s, re * s + im * c)
+                for p in range(2):
+                    start = p * band + h * width
+                    turned[m, pl.ds(first, size), start : start + width] = pair[p].astype(
+                        jnp.bfloat16
+                    )
+
+    edge_row = lax.broadcasted_iota(jnp.int32, (EDGE, width), 0)
+    has_edge = jnp.where(epoch == epoch_count - 1, 1.0, 0.0)
+
+    def sections(cut, tiles):
+        rows = cut_rows + (EDGE if cut == cuts - 1 else 0)
+        stack = [turned[tile, cut * cut_rows : cut * cut_rows + rows, :] for tile in tiles]
+        moved = jnp.dot(
+            jnp.concatenate(stack, 0), second_ref[...], preferred_element_type=jnp.float32
         )
-        return both.astype(jnp.bfloat16)
-
-    full_ref[epoch * half + mine] = fold(0)
-    for j in range(1, epoch_count):
-        epoch_copy(0, j).start()
-
-    def send(k, carry):
-        folded[k] = fold(k)
-        tile_copy(k).start()
-        return carry
-
-    lax.fori_loop(1, half, send, 0)
-
-    def forward(k, carry):
-        tile_copy(k).wait_recv()
+        blocks = []
+        for i in range(len(tiles)):
+            pieces = [
+                moved[i * rows : (i + 1) * rows, q * width : (q + 1) * width] for q in range(parts)
+            ]
+            block = [piece[:cut_rows] for piece in pieces]
+            if cut == cuts - 1:
+                edge = jnp.zeros((EDGE, width), jnp.float32)
+                for q, piece in enumerate(pieces):
+                    edge = jnp.where(edge_row == q, piece[cut_rows : cut_rows + 1] * has_edge, edge)
+                block.append(edge)
+            blocks.append(jnp.concatenate(block, 0))
+        return blocks
+
+    def forward(cut, first, last):
+        def step(k, carry):
+            tile_copy(cut, k).wait_recv()
+            for j in range(1, epoch_count):
+                epoch_copy(cut, k, j).start()
+            return carry
+
+        lax.fori_loop(first, last, step, 0)
+
+    early = min(3, half)
+    for cut in range(cuts):
+
+        def row_group(i, carry):
+            transform(pl.multiple_of(i * group, group), group)
+            return carry
+
+        lax.fori_loop(cut * cut_rows // group, (cut + 1) * cut_rows // group, row_group, 0)
+        if cut == cuts - 1:
+            transform(rows_here, EDGE)
+        if cut == 0:
+            pl.semaphore_wait(barrier, half + epoch_count - 1)
+        else:
+            forward(cut - 1, 1, early)
+        for b in range(0, half, batch):
+            tiles = [lax.rem(mine + b + i, half) * 2 + 1 - side for i in range(batch)]
+            for i, block in enumerate(sections(cut, tiles)):
+                given[b + i, rows_of(cut), :] = block.astype(jnp.bfloat16)
+                partner_copy(cut, b + i).start()
+        for b in range(0, half, batch):
+            tiles = [lax.rem(mine + b + i, half) * 2 + side for i in range(batch)]
+            for i, block in enumerate(sections(cut, tiles)):
+                k = b + i
+                partner_copy(cut, k).wait_recv()
+                both = (block + landed[k, rows_of(cut), :].astype(jnp.float32)).astype(jnp.bfloat16)
+                if k == 0:
+                    full[epoch * half + mine, rows_of(cut), :] = both
+                    for j in range(1, epoch_count):
+                        epoch_copy(cut, 0, j).start()
+                else:
+                    folded[k, rows_of(cut), :] = both
+                    tile_copy(cut, k).start()
+    for cut in range(cuts):
+        forward(cut, early if cut < cuts - 1 else 1, half)
+
+    def mix_rows(e, cut, first, edges=None):
+        for h in range(chunks):
+            values = []
+            for j in range(half):
+                value = tuple(
+                    full[
+                        e * half + j, pl.ds((cut * parts + h * 2 + p) * cut_rows + first, group), :
+                    ].astype(jnp.float32)
+                    for p in range(2)
+                )
+                values.append(epoch_turn(value, j, epoch, epoch_count))
+            done = dft(values + [None] * half, kept)
+            if edges is not None:
+                top = lax.broadcasted_iota(jnp.int32, (group, width), 0) == 0
+                done = [
+                    tuple(a + jnp.where(top, b, 0.0) for a, b in zip(part, edge))
+                    for part, edge in zip(done, edges[h])
+                ]
+            for c, part in enumerate(done):
+                for p in range(2):
+                    row = pl.multiple_of(
+                        p * band + e * rows_here + cut * cut_rows + first, group
+                    )
+                    mixed_ref[c, pl.ds(row, group), h * width : (h + 1) * width] = part[p].astype(
+                        jnp.bfloat16
+                    )
+
+    def mix(e, cut):
+        def step(i, carry):
+            mix_rows(e, cut, pl.multiple_of(i * group, group))
+            return carry
+
+        lax.fori_loop(0, cut_rows // group, step, 0)
+
+    for cut in range(cuts):
+        mix(epoch, cut)
+    for cut in range(cuts):
         for j in range(1, epoch_count):
-            epoch_copy(k, j).start()
-        return carry
-
-    lax.fori_loop(1, half, forward, 0)
-
-    def finish(k, carry):
-        tile_copy(k).wait_send()
-        return carry
-
-    lax.fori_loop(1, half, finish, 0)
-
-    def settle(k, carry):
-        partner_copy(k).wait_send()
-        for j in range(1, epoch_count):
-            epoch_copy(k, j).wait()
-        return carry
-
-    lax.fori_loop(0, half, settle, 0)
-
-
-def image_kernel(
-    sizes, image_scale, epoch_ref, full_ref, last_ref, rows_ref, cols_ref, out_ref, mixed
-):
-    tile_count, epoch_count = sizes
-    half, kept = tile_count // 2, tile_count // epoch_count
-    width = full_ref.shape[2]
-    block_len = out_ref.shape[1]
-    chunks = block_len // width
-    parts = 2 * chunks
-    rows_here = block_len // epoch_count
-    group = min(16, rows_here)
-    epoch = epoch_ref[0]
-
-    @pl.when(pl.program_id(0) == 0)
+
+            def arrive(k, carry, cut=cut, j=j):
+                epoch_copy(cut, k, j).wait_recv()
+                return carry
+
+            lax.fori_loop(0, half, arrive, 0)
+            mix(lax.rem(epoch + epoch_count - j, epoch_count), cut)
+
+    edges = []
+    for h in range(chunks):
+        values = [None]
+        for j in range(half):
+            block = full[(epoch_count - 1) * half + j, cuts * parts * cut_rows :, :]
+            block = block.astype(jnp.float32)
+            value = tuple(block[h * 2 + p : h * 2 + p + 1] for p in range(2))
+            values.append(epoch_turn(value, j + 1, epoch, epoch_count))
+        edges.append(dft(values + [None] * (tile_count - half - 1), kept))
+    mix_rows(0, 0, 0, edges)
+
+    for cut in range(cuts):
+
+        def finish(k, carry, cut=cut):
+            tile_copy(cut, k).wait_send()
+            return carry
+
+        lax.fori_loop(1, half, finish, 0)
+
+        def settle(k, carry, cut=cut):
+            partner_copy(cut, k).wait_send()
+            for j in range(1, epoch_count):
+                epoch_copy(cut, k, j).wait_send()
+            return carry
+
+        lax.fori_loop(0, half, settle, 0)
+
+
+def image_kernel(image_scale, epoch_ref, mixed_ref, last_ref, rows_ref, cols_ref, out_ref, tall):
+    c = pl.program_id(0)
+
+    @pl.when(c == 0)
     def _():
-        def per_group(e, first, edges):
-            for h in range(chunks):
-                values = []
-                for j in range(half):
-                    value = tuple(
-                        full_ref[
-                            e * half + j, pl.ds((h * 2 + p) * rows_here + first, group), :
-                        ].astype(jnp.float32)
-                        for p in range(2)
-                    )
-                    values.append(epoch_turn(value, j, epoch, epoch_count))
-                done = dft(values + [None] * half, kept)
-                if edges is not None:
-                    top = lax.broadcasted_iota(jnp.int32, (group, width), 0) == 0
-                    done = [
-                        tuple(a + jnp.where(top, b, 0.0) for a, b in zip(part, edge))
-                        for part, edge in zip(done, edges[h])
-                    ]
-                for c, part in enumerate(done):
-                    for p in range(2):
-                        row = p * block_len + e * rows_here + first
-                        if not isinstance(row, int):
-                            row = pl.multiple_of(row, group)
-                        mixed[c, pl.ds(row, group), h * width : (h + 1) * width] = part[p].astype(
-                            jnp.bfloat16
-                        )
-
-        edges = []
-        for h in range(chunks):
-            values = [None]
-            for j in range(half):
-                block = full_ref[(epoch_count - 1) * half + j, parts * rows_here :, :].astype(
-                    jnp.float32
-                )
-                value = tuple(block[h * 2 + p : h * 2 + p + 1] for p in range(2))
-                values.append(epoch_turn(value, j + 1, epoch, epoch_count))
-            edges.append(dft(values + [None] * (tile_count - half - 1), kept))
-        per_group(0, 0, edges)
-        for e in range(epoch_count):
-
-            def step(i, carry, e=e):
-                per_group(e, pl.multiple_of(i * group, group), None)
-                return carry
-
-            lax.fori_loop(1 if e == 0 else 0, rows_here // group, step, 0)
-
-    c = pl.program_id(0)
-    pixels = jnp.dot(last_ref[0], mixed[c], preferred_element_type=jnp.float32)
-    out_ref[0] = pixels * (rows_ref[0] * image_scale) * cols_ref[...]
+        tall[...] = jnp.transpose(rows_ref[...]) * image_scale
+
+    lane = lax.broadcasted_iota(jnp.int32, tall.shape, 1)
+    factor = jnp.sum(jnp.where(lane == c, tall[...], 0.0), 1, keepdims=True)
+    pixels = jnp.dot(last_ref[0], mixed_ref[c], preferred_element_type=jnp.float32)
+    out_ref[0] = pixels * factor * cols_ref[...]
 
 
 def turns(product, modulus):
@@ -614,73 +639,72 @@
         owners,
         row_offsets,
         col_offsets,
-        coords.reshape(n_slots, 2 * n_samples),
-        samples.reshape(n_slots, 2 * n_samples),
+        coords,
+        samples,
     )
 
     lane_blocks = tile_count * band // LANES
-    block_shape = (parts * rows_here + EDGE, width)
-    own = pl.pallas_call(
-        functools.partial(band_kernel, sizes),
-        out_shape=jax.ShapeDtypeStruct((tile_count, *block_shape), jnp.bfloat16),
-        in_specs=[pl.BlockSpec(memory_space=pltpu.SMEM)] + vmem(4),
+    acc = pl.pallas_call(
+        functools.partial(place_kernel, sizes),
+        out_shape=jax.ShapeDtypeStruct(
+            (2, lane_blocks + 1, rows_here + 3 * SUB, LANES), jnp.float32
+        ),
+        in_specs=[pl.BlockSpec(memory_space=pltpu.SMEM)] + vmem(1),
         out_specs=vmem(1)[0],
         scratch_shapes=[
-            pltpu.VMEM((2, lane_blocks + 1, rows_here + 3 * SUB, LANES), jnp.float32),
-            pltpu.VMEM((tile_count, rows_here + EDGE, 2 * band), jnp.bfloat16),
             pltpu.SMEM((epoch_count * tile_count * capacity + UNROLL,), jnp.int32),
             pltpu.VMEM((epoch_count, SUB, LANES), jnp.float32),
         ],
         compiler_params=pltpu.CompilerParams(vmem_limit_bytes=VMEM_BYTES),
-        name="band_rows",
-    )(meta, pool, jnp.asarray(turn_cos), jnp.asarray(turn_sin), jnp.asarray(second))
-
-    half_sems = pltpu.SemaphoreType.DMA((half,))
-    epoch_sems = pltpu.SemaphoreType.DMA(((epoch_count - 1) * half,))
-    full = pl.pallas_call(
-        functools.partial(swap_kernel, tile_count, epoch_count),
-        out_shape=jax.ShapeDtypeStruct((epoch_count * half, *block_shape), jnp.bfloat16),
-        in_specs=vmem(1),
+        name="place_slots",
+    )(meta, pool)
+
+    cuts = 2 if rows_here % 32 == 0 else 1
+    block_shape = (parts * rows_here + EDGE, width)
+    sems = [pltpu.SemaphoreType.DMA((cuts * half,))] * 4
+    sems += [pltpu.SemaphoreType.DMA((cuts * (epoch_count - 1) * half,))] * 2
+    mixed = pl.pallas_call(
+        functools.partial(swap_kernel, (tile_count, epoch_count, band), cuts),
+        out_shape=jax.ShapeDtypeStruct((kept, 2 * band, band), jnp.bfloat16),
+        in_specs=vmem(4),
         out_specs=vmem(1)[0],
         scratch_shapes=[
+            pltpu.VMEM((tile_count, rows_here + EDGE, 2 * band), jnp.bfloat16),
             pltpu.VMEM((half, *block_shape), jnp.bfloat16),
             pltpu.VMEM((half, *block_shape), jnp.bfloat16),
-            half_sems,
-            half_sems,
-            half_sems,
-            half_sems,
-            epoch_sems,
-            epoch_sems,
+            pltpu.VMEM((half, *block_shape), jnp.bfloat16),
+            pltpu.VMEM((epoch_count * half, *block_shape), jnp.bfloat16),
+            *sems,
         ],
         compiler_params=pltpu.CompilerParams(
             vmem_limit_bytes=VMEM_BYTES, collective_id=0, has_side_effects=True
         ),
         name="swap_rows",
-    )(own)
+    )(acc, jnp.asarray(turn_cos), jnp.asarray(turn_sin), jnp.asarray(second))
 
     image_scale = math.sqrt(n_slots) / (64.0 * tile_count * math.sqrt(epoch_count))
     return pl.pallas_call(
-        functools.partial(image_kernel, (tile_count, epoch_count), image_scale),
+        functools.partial(image_kernel, image_scale),
         grid_spec=pltpu.PrefetchScalarGridSpec(
             num_scalar_prefetch=1,
             grid=(kept,),
             in_specs=[
                 pl.BlockSpec(memory_space=pltpu.VMEM),
                 pl.BlockSpec((1, band, 2 * band), lambda c, e: (e[0] * kept + c, 0, 0)),
-                pl.BlockSpec((1, band, 1), lambda c, e: (c, 0, 0)),
+                pl.BlockSpec((kept, band), lambda c, e: (0, 0)),
                 pl.BlockSpec((1, band), lambda c, e: (0, 0)),
             ],
             out_specs=pl.BlockSpec((1, band, band), lambda c, e: (c, 0, 0)),
-            scratch_shapes=[pltpu.VMEM((kept, 2 * band, band), jnp.bfloat16)],
+            scratch_shapes=[pltpu.VMEM((band, kept), jnp.float32)],
         ),
         out_shape=jax.ShapeDtypeStruct((kept, band, band), jnp.float32),
         compiler_params=pltpu.CompilerParams(vmem_limit_bytes=VMEM_BYTES),
         name="image_rows",
     )(
         lax.axis_index("epoch").astype(jnp.int32)[None],
-        full,
+        mixed,
         jnp.asarray(last),
-        taper_rows[:, :, None],
+        taper_rows,
         taper_cols[None, :],
     )
 

time: 111 us -> 101 us (0.910)
  the two profiles are of different devices: /device:TPU:27 before, /device:TPU:8 now
where the time goes in v2:
time: 101 us; the launch traced here: 100 us
  Pallas kernels  100 us (99%)
    pallas_call x1, Pallas kernels, body(): pl.pallas_call(functools.partial(swap_kernel, (tile_count, epoch_count, b...  51.1 us
    pallas_call x1, Pallas kernels, body(): pl.pallas_call(functools.partial(grid_kernel, sizes), out_shape=[jax.Shap...  30.7 us
    pallas_call x1, Pallas kernels, body(): pl.pallas_call(functools.partial(place_kernel, sizes), out_shape=jax.Shap...  11.2 us
    pallas_call x1, Pallas kernels, body(): pl.pallas_call(functools.partial(image_kernel, image_scale), grid_spec=pl...  7.32 us

profile of v2, /device:TPU:8, one launch (start us, length us, event | category | flops | bytes accessed | tf_op | source)
XLA Modules:
  0.0 100.4 jit_solution(6602780389034002963)
XLA Ops:
  0.0 30.7 %grid_slots.1 = (bf16[32,176,128]{2,1,0:T(8,128)(2,1)}, s32[4,8,128]{2,1,0:T(8,128)}) custom-call(s32[1,128]{1,0:T(1,128)} %owner_ref.1, s32[1,128]{1,0:T(1,128)} %row_ref.1, s32[1,128]{1,0:T(1,128)} %col_ref.1, f32[1,128,2,256]{3,2,1,0:T(2,128)} %coords_ref.1, bf16[1,128,2,256]{3,2,1,0:T(2,128)(2,1)} %samples_ref.1), custom_call_target="tpu_custom_call" | custom-call | tf_op jit(solution)/shard_map/grid_slots/pallas_call | solution.py:618
  30.7 11.2 %place_slots.1.acc_ref = f32[2,33,224,128]{3,2,1,0:T(8,128)} custom-call(s32[4,8,128]{2,1,0:T(8,128)} %get-tuple-element.7.meta_ref, bf16[32,176,128]{2,1,0:T(8,128)(2,1)} %get-tuple-element.8.pool_ref), custom_call_target="tpu_custom_call" | custom-call | tf_op jit(solution)/shard_map/place_slots/pallas_call | solution.py:647
  41.9 51.1 %swap_rows.1.mixed_ref = bf16[8,512,256]{2,1,0:T(8,128)(2,1)} custom-call(f32[2,33,224,128]{3,2,1,0:T(8,128)} %place_slots.1.acc_ref, f32[16,256]{1,0:T(8,128)} %constant.14.clone.cos_ref, f32[16,256]{1,0:T(8,128)} %constant.15.clone.sin_ref, bf16[512,512]{1,0:T(8,128)(2,1)} %constant.16.clone.second_ref), custom_call_target="tpu_custom_call" | custom-call | tf_op jit(solution)/shard_map/swap_rows/pallas_call | solution.py:666
  93.0 7.3 %image_rows.1 = f32[8,256,256]{2,1,0:T(8,128)} custom-call(s32[1]{0:T(128)} %bitcast.epoch_ref, bf16[8,512,256]{2,1,0:T(8,128)(2,1)} %swap_rows.1.mixed_ref, bf16[16,256,512]{2,1,0:T(8,128)(2,1)} %constant.17.clone.last_ref, f32[8,256]{1,0:T(8,128)} %rows_ref.1, f32[1,256]{1,0:T(1,128)} %bitcast.2), custom_call_target="tpu_custom_call" | custom-call | tf_op jit(solution)/shard_map/image_rows/pallas_call | solution.py:686

commit v3 on v2

--- a/solution.py
+++ b/solution.py
@@ -14,6 +14,7 @@
 EDGE = 16
 FIELDS = 8
 UNROLL = 8
+BEHIND = 3
 VMEM_BYTES = 56 * 1024 * 1024
 MESH = pl.DeviceIdType.MESH
 
@@ -89,8 +90,33 @@
     return re * c - im * s, re * s + im * c
 
 
+def exclusive(a, b, count):
+    total = 0
+    for bit in range(count.bit_length() - 1):
+        x, y = lax.rem(a // (1 << bit), 2), lax.rem(b // (1 << bit), 2)
+        total += (x + y - 2 * x * y) * (1 << bit)
+    return total
+
+
+def near_and_far(i, count):
+    return jnp.where(
+        i == count - 2,
+        count - 1,
+        jnp.where(lax.rem(i, 2) == 0, 1 + i // 2, count // 2 + i // 2),
+    )
+
+
 def grid_kernel(
-    sizes, owner_ref, row_ref, col_ref, coords_ref, samples_ref, pool_ref, meta_ref, *scratch
+    sizes,
+    owner_ref,
+    row_ref,
+    col_ref,
+    coords_ref,
+    samples_ref,
+    pool_ref,
+    list_ref,
+    weight_ref,
+    *scratch,
 ):
     tile_count, epoch_count, capacity, lane_step, band = sizes
     packed, points, t_send, t_recv, x_send, x_recv = scratch
@@ -185,7 +211,7 @@
             ).astype(jnp.bfloat16)
 
     def tile_copy(k):
-        peer = lax.rem(me + k, tile_count)
+        peer = exclusive(me, k, tile_count)
         return pltpu.make_async_remote_copy(
             src_ref=packed.at[peer],
             dst_ref=pool_ref.at[me],
@@ -196,7 +222,7 @@
         )
 
     def epoch_copy(k, j):
-        origin = lax.rem(me + tile_count - k, tile_count)
+        origin = exclusive(me, k, tile_count)
         return pltpu.make_async_remote_copy(
             src_ref=pool_ref.at[origin],
             dst_ref=pool_ref.at[j * tile_count + origin],
@@ -211,20 +237,35 @@
     for j in range(1, epoch_count):
         epoch_copy(0, j).start()
 
-    def send(k, carry):
-        make(lax.rem(me + k, tile_count))
+    def send(i):
+        k = near_and_far(i, tile_count)
+        make(exclusive(me, k, tile_count))
         tile_copy(k).start()
-        return carry
-
-    lax.fori_loop(1, tile_count, send, 0)
-
-    def forward(k, carry):
+
+    def forward(i):
+        k = near_and_far(i, tile_count)
         tile_copy(k).wait_recv()
         for j in range(1, epoch_count):
             epoch_copy(k, j).start()
+
+    behind = min(BEHIND, tile_count - 1)
+
+    def first_sends(i, carry):
+        send(i)
         return carry
 
-    lax.fori_loop(1, tile_count, forward, 0)
+    def both(i, carry):
+        send(i)
+        forward(i - behind)
+        return carry
+
+    def last_forwards(i, carry):
+        forward(i)
+        return carry
+
+    lax.fori_loop(0, behind, first_sends, 0)
+    lax.fori_loop(behind, tile_count - 1, both, 0)
+    lax.fori_loop(tile_count - 1 - behind, tile_count - 1, last_forwards, 0)
 
     def sent_all(k, carry):
         tile_copy(k).wait_send()
@@ -232,94 +273,108 @@
 
     lax.fori_loop(1, tile_count, sent_all, 0)
 
-    def crossed(k, carry):
-        for j in range(1, epoch_count):
-            epoch_copy(k, j).wait()
-        return carry
-
-    lax.fori_loop(0, tile_count, crossed, 0)
-
-    for j in range(epoch_count):
+    rows_here = band // epoch_count
+    first_row = (epoch * rows_here - SUB).astype(jnp.float32)
+    spots = groups * LANES
+    below = lax.broadcasted_iota(jnp.int32, (LANES, LANES), 0) < lax.broadcasted_iota(
+        jnp.int32, (LANES, LANES), 1
+    )
+    below = jnp.where(below, 1.0, 0.0).astype(jnp.bfloat16)
+    spot = lax.broadcasted_iota(jnp.int32, (spots, LANES), 0).astype(jnp.float32)
+    lanes = lax.broadcasted_iota(jnp.int32, (1, LANES), 1)
+    field = lax.broadcasted_iota(jnp.int32, (FIELDS, spots), 0)
+
+    def list_slots(j):
+        found, held = jnp.zeros((1, 1), jnp.float32), jnp.zeros((1, 1), jnp.float32)
+        gathered = jnp.zeros((EDGE, spots), jnp.float32)
         for g in range(groups):
             total = jnp.zeros((EDGE, LANES), jnp.float32)
             for s in range(g * per_meta, min(tile_count, (g + 1) * per_meta)):
                 total += pool_ref[j * tile_count + s, capacity * slot_rows :, :].astype(jnp.float32)
-            meta_ref[j * groups + g] = total[:FIELDS].astype(jnp.int32)
-
-
-def place_kernel(sizes, meta_ref, pool_ref, acc, wanted, scale):
-    tile_count, epoch_count, capacity, lane_step, band = sizes
-    epoch = lax.axis_index("epoch")
-    lane_blocks, acc_rows = acc.shape[1] - 1, acc.shape[2]
-    rows_here = band // epoch_count
-    spare = acc_rows - SUB
+            valid, row = total[0:1], total[1:2] - first_row
+            inside = (valid > 0) & (row > 0) & (row < rows_here + SUB)
+            mask = jnp.where(inside, 1.0, 0.0)
+            order = jnp.dot(
+                mask.astype(jnp.bfloat16), below, preferred_element_type=jnp.float32
+            )
+            chosen = spot == jnp.where(inside, order + found, -1.0)
+            source = (g * per_meta + lanes // lane_step).astype(jnp.float32)
+            place = (lanes % lane_step).astype(jnp.float32)
+            rows = [source, row, total[2:3], total[3:4], place]
+            rows = jnp.concatenate(rows + [jnp.zeros_like(row)] * (EDGE - len(rows)), 0)
+            gathered += lax.dot_general(
+                rows.astype(jnp.bfloat16),
+                jnp.where(chosen, 1.0, 0.0).astype(jnp.bfloat16),
+                (((1,), (1,)), ((), ())),
+                preferred_element_type=jnp.float32,
+            )
+            found += jnp.sum(mask, 1, keepdims=True)
+            held += jnp.sum(valid, 1, keepdims=True)
+        listed = jnp.where(field == FIELDS - 1, found, gathered[:FIELDS])
+        list_ref[j] = listed.astype(jnp.int32)
+        weight_ref[j] = jnp.broadcast_to(1.0 / jnp.maximum(held, 1.0), (FIELDS, LANES))
+
+    list_slots(0)
+    for j in range(1, epoch_count):
+
+        def arrived(k, carry, j=j):
+            epoch_copy(k, j).wait_recv()
+            return carry
+
+        lax.fori_loop(0, tile_count, arrived, 0)
+        list_slots(j)
+
+    def crossed(k, carry):
+        for j in range(1, epoch_count):
+            epoch_copy(k, j).wait_send()
+        return carry
+
+    lax.fori_loop(0, tile_count, crossed, 0)
+
+
+def place_kernel(tile_count, list_ref, weight_ref, pool_ref, acc):
+    acc_rows = acc.shape[2]
     slot_rows = SUB // 2
-    per_meta = LANES // lane_step
-    groups = -(-tile_count // per_meta)
-    first_row = epoch * rows_here - SUB
 
     def clear(i, carry):
         acc[0, i] = jnp.zeros((acc_rows, LANES), jnp.float32)
         acc[1, i] = jnp.zeros((acc_rows, LANES), jnp.float32)
         return carry
 
-    lax.fori_loop(0, lane_blocks + 1, clear, 0)
-
-    found = jnp.int32(0)
-    for e in range(epoch_count):
-        held = jnp.int32(0)
-        for g in range(groups):
-            at = e * groups + g
-
-            def look(s, carry, at=at):
-                found, held = carry
-                for k in range(capacity):
-                    lane = s * lane_step + k
-                    valid = meta_ref[at, 0, lane]
-                    row = meta_ref[at, 1, lane] - first_row
-                    inside = (valid > 0) & (row > 0) & (row < rows_here + SUB)
-                    wanted[found] = at * LANES + lane
-                    found += jnp.where(inside, 1, 0)
-                    held += valid
-                return found, held
-
-            count = min(tile_count - g * per_meta, per_meta)
-            found, held = lax.fori_loop(0, count, look, (found, held))
-        scale[e] = 1.0 / jnp.full((SUB, LANES), jnp.maximum(held, 1), jnp.int32).astype(jnp.float32)
-    for k in range(UNROLL):
-        wanted[found + k] = -1
-
-    shape = (SUB, 2 * LANES)
-    steps = lax.broadcasted_iota(jnp.int32, shape, 1) - lax.broadcasted_iota(jnp.int32, shape, 0)
-
-    def per_batch(b, carry):
-        placed = []
-        for k in range(UNROLL):
-            entry = wanted[b * UNROLL + k]
-            index = jnp.maximum(entry, 0)
-            at, lane = index // LANES, lax.rem(index, LANES)
-            e, g = at // groups, lax.rem(at, groups)
-            source = e * tile_count + g * per_meta + lane // lane_step
-            row = jnp.where(entry < 0, spare, meta_ref[at, 1, lane] - first_row)
-            block = meta_ref[at, 2, lane]
-            start = meta_ref[at, 3, lane]
-            first = pl.multiple_of(lax.rem(lane, lane_step) * slot_rows, slot_rows)
-            data = pool_ref[source, pl.ds(first, slot_rows), :]
-            parts = jnp.concatenate(
-                [data[:, i * SUB : (i + 1) * SUB] for i in (0, 2, 1, 3)], 0
-            )
-            select = jnp.where(steps == start, 1.0, 0.0).astype(jnp.bfloat16)
-            window = jnp.dot(parts, select, preferred_element_type=jnp.float32)
-            placed.append((row, block, scale[e], window))
-        for row, block, factor, window in placed:
-            for p in range(2):
-                for h in range(2):
-                    acc[p, block + h, pl.ds(row, SUB), :] += (
-                        window[p * SUB : (p + 1) * SUB, h * LANES : (h + 1) * LANES] * factor
-                    )
-        return carry
-
-    lax.fori_loop(0, (found + UNROLL - 1) // UNROLL, per_batch, 0)
+    lax.fori_loop(0, acc.shape[1], clear, 0)
+    lanes = lax.broadcasted_iota(jnp.int32, (slot_rows, LANES), 1)
+
+    for e in range(list_ref.shape[0]):
+        weight = jnp.concatenate([weight_ref[e]] * (slot_rows // FIELDS), 0)
+
+        def per_batch(b, carry, e=e, weight=weight):
+            placed = []
+            for k in range(UNROLL):
+                at = b * UNROLL + k
+                source, row, block, start, place = (list_ref[e, f, at] for f in range(5))
+                first = pl.multiple_of(place * slot_rows, slot_rows)
+                data = pool_ref[e * tile_count + source, pl.ds(first, slot_rows), :]
+                data = data.astype(jnp.float32) * weight
+                turned = [
+                    pltpu.roll(data, lax.rem(start + (LANES - i * SUB), LANES), 1)
+                    for i in range(4)
+                ]
+                near = (lanes >= start) & (lanes < start + SUB)
+                far = lanes < start + SUB - LANES
+                windows = [
+                    jnp.concatenate([jnp.where(mask, turned[i], 0.0) for i in (p, 2 + p)], 0)
+                    for p in range(2)
+                    for mask in (near, far)
+                ]
+                placed.append((row, block, windows))
+            for row, block, windows in placed:
+                spots = [(p, block + h, pl.ds(row, SUB)) for p in range(2) for h in range(2)]
+                sums = [acc[spot] + window for spot, window in zip(spots, windows)]
+                for spot, total in zip(spots, sums):
+                    acc[spot] = total
+            return carry
+
+        lax.fori_loop(0, (list_ref[e, FIELDS - 1, 0] + UNROLL - 1) // UNROLL, per_batch, 0)
 
 
 def swap_kernel(sizes, cuts, acc_ref, cos_ref, sin_ref, second_ref, mixed_ref, *scratch):
@@ -342,7 +397,7 @@
     barrier = pltpu.get_barrier_semaphore()
 
     def greet(k, carry):
-        peer = lax.rem(mine + k, half) * 2 + side
+        peer = exclusive(mine, k, half) * 2 + side
         pl.semaphore_signal(barrier, inc=1, device_id={"tile": peer}, device_id_type=MESH)
         return carry
 
@@ -372,12 +427,12 @@
             dst_ref=full.at[epoch * half + mine, rows_of(cut)],
             send_sem=t_send.at[cut * half + k],
             recv_sem=t_recv.at[cut * half + k],
-            device_id={"tile": lax.rem(mine + k, half) * 2 + side},
+            device_id={"tile": exclusive(mine, k, half) * 2 + side},
             device_id_type=MESH,
         )
 
     def epoch_copy(cut, k, j):
-        origin = epoch * half + lax.rem(mine + half - k, half)
+        origin = epoch * half + exclusive(mine, k, half)
         at = (cut * (epoch_count - 1) + j - 1) * half + k
         return pltpu.make_async_remote_copy(
             src_ref=full.at[origin, rows_of(cut)],
@@ -434,38 +489,42 @@
             blocks.append(jnp.concatenate(block, 0))
         return blocks
 
-    def forward(cut, first, last):
-        def step(k, carry):
-            tile_copy(cut, k).wait_recv()
-            for j in range(1, epoch_count):
-                epoch_copy(cut, k, j).start()
-            return carry
-
-        lax.fori_loop(first, last, step, 0)
-
-    early = min(3, half)
+    def forward(cut, k):
+        tile_copy(cut, k).wait_recv()
+        for j in range(1, epoch_count):
+            epoch_copy(cut, k, j).start()
+
+    order = [0] + [k for pair in zip(range(1, half), range(half // 2, half)) for k in pair]
+    order = order[: 1 + 2 * (half // 2 - 1)] + [half - 1] if half > 1 else [0]
+    pending = []
     for cut in range(cuts):
 
         def row_group(i, carry):
             transform(pl.multiple_of(i * group, group), group)
             return carry
 
-        lax.fori_loop(cut * cut_rows // group, (cut + 1) * cut_rows // group, row_group, 0)
+        if not pending:
+            steps = cut_rows // group
+            lax.fori_loop(cut * steps, (cut + 1) * steps, row_group, 0)
+        else:
+            for i in range(cut_rows // group):
+                transform(cut * cut_rows + i * group, group)
+                if pending:
+                    forward(*pending.pop(0))
         if cut == cuts - 1:
             transform(rows_here, EDGE)
         if cut == 0:
             pl.semaphore_wait(barrier, half + epoch_count - 1)
-        else:
-            forward(cut - 1, 1, early)
         for b in range(0, half, batch):
-            tiles = [lax.rem(mine + b + i, half) * 2 + 1 - side for i in range(batch)]
-            for i, block in enumerate(sections(cut, tiles)):
-                given[b + i, rows_of(cut), :] = block.astype(jnp.bfloat16)
-                partner_copy(cut, b + i).start()
+            ks = order[b : b + batch]
+            tiles = [exclusive(mine, k, half) * 2 + 1 - side for k in ks]
+            for k, block in zip(ks, sections(cut, tiles)):
+                given[k, rows_of(cut), :] = block.astype(jnp.bfloat16)
+                partner_copy(cut, k).start()
         for b in range(0, half, batch):
-            tiles = [lax.rem(mine + b + i, half) * 2 + side for i in range(batch)]
-            for i, block in enumerate(sections(cut, tiles)):
-                k = b + i
+            ks = order[b : b + batch]
+            tiles = [exclusive(mine, k, half) * 2 + side for k in ks]
+            for k, block in zip(ks, sections(cut, tiles)):
                 partner_copy(cut, k).wait_recv()
                 both = (block + landed[k, rows_of(cut), :].astype(jnp.float32)).astype(jnp.bfloat16)
                 if k == 0:
@@ -475,8 +534,11 @@
                 else:
                     folded[k, rows_of(cut), :] = both
                     tile_copy(cut, k).start()
-    for cut in range(cuts):
-        forward(cut, early if cut < cuts - 1 else 1, half)
+                if cut > 0 and pending:
+                    forward(*pending.pop(0))
+        pending += [(cut, k) for k in order[1:]]
+    for cut, k in pending:
+        forward(cut, k)
 
     def mix_rows(e, cut, first, edges=None):
         for h in range(chunks):
@@ -611,18 +673,19 @@
     turn_cos, turn_sin, second, last = tables
     sizes = (tile_count, epoch_count, capacity, lane_step, band)
     block_rows = capacity * SUB // 2 + EDGE
-    meta_rows = epoch_count * -(-tile_count // (LANES // lane_step))
+    spots = -(-tile_count // (LANES // lane_step)) * LANES
 
     tile_sems = pltpu.SemaphoreType.DMA((tile_count,))
     epoch_sems = pltpu.SemaphoreType.DMA(((epoch_count - 1) * tile_count,))
-    pool, meta = pl.pallas_call(
+    pool, slot_list, weights = pl.pallas_call(
         functools.partial(grid_kernel, sizes),
         out_shape=[
             jax.ShapeDtypeStruct((epoch_count * tile_count, block_rows, LANES), jnp.bfloat16),
-            jax.ShapeDtypeStruct((meta_rows, FIELDS, LANES), jnp.int32),
+            jax.ShapeDtypeStruct((epoch_count, FIELDS, spots), jnp.int32),
+            jax.ShapeDtypeStruct((epoch_count, FIELDS, LANES), jnp.float32),
         ],
         in_specs=vmem(5),
-        out_specs=vmem(2),
+        out_specs=vmem(3),
         scratch_shapes=[
             pltpu.VMEM((tile_count, block_rows, LANES), jnp.bfloat16),
             pltpu.VMEM((tile_count, 2 * lane_step, 2 * n_samples), jnp.float32),
@@ -645,19 +708,15 @@
 
     lane_blocks = tile_count * band // LANES
     acc = pl.pallas_call(
-        functools.partial(place_kernel, sizes),
+        functools.partial(place_kernel, tile_count),
         out_shape=jax.ShapeDtypeStruct(
-            (2, lane_blocks + 1, rows_here + 3 * SUB, LANES), jnp.float32
+            (2, lane_blocks + 1, rows_here + 2 * SUB, LANES), jnp.float32
         ),
-        in_specs=[pl.BlockSpec(memory_space=pltpu.SMEM)] + vmem(1),
+        in_specs=[pl.BlockSpec(memory_space=pltpu.SMEM)] + vmem(2),
         out_specs=vmem(1)[0],
-        scratch_shapes=[
-            pltpu.SMEM((epoch_count * tile_count * capacity + UNROLL,), jnp.int32),
-            pltpu.VMEM((epoch_count, SUB, LANES), jnp.float32),
-        ],
         compiler_params=pltpu.CompilerParams(vmem_limit_bytes=VMEM_BYTES),
         name="place_slots",
-    )(meta, pool)
+    )(slot_list, weights, pool)
 
     cuts = 2 if rows_here % 32 == 0 else 1
     block_shape = (parts * rows_here + EDGE, width)

time: 101 us -> 90 us (0.89)
  the two profiles are of different devices: /device:TPU:8 before, /device:TPU:0 now
where the time goes in v3:
time: 90 us
  Pallas kernels  90 us (100%)
    pallas_call x1, Pallas kernels, body(): pl.pallas_call(functools.partial(swap_kernel, (tile_count, epoch_count, b...  42.2 us
    pallas_call x1, Pallas kernels, body(): pl.pallas_call(functools.partial(grid_kernel, sizes), out_shape=[jax.Shap...  32.6 us
    pallas_call x1, Pallas kernels, body(): pl.pallas_call(functools.partial(place_kernel, tile_count), out_shape=jax...  7.88 us
    pallas_call x1, Pallas kernels, body(): pl.pallas_call(functools.partial(image_kernel, image_scale), grid_spec=pl...  7.32 us

profile of v3, /device:TPU:0, one launch (start us, length us, event | category | flops | bytes accessed | tf_op | source)
XLA Modules:
  0.0 90.0 jit_solution(3800092812218893931)
XLA Ops:
  0.0 32.6 %grid_slots.1 = (bf16[32,176,128]{2,1,0:T(8,128)(2,1)}, s32[2,8,256]{2,1,0:T(8,128)}, f32[2,8,128]{2,1,0:T(8,128)}) custom-call(s32[1,128]{1,0:T(1,128)} %owner_ref.1, s32[1,128]{1,0:T(1,128)} %row_ref.1, s32[1,128]{1,0:T(1,128)} %col_ref.1, f32[1,128,2,256]{3,2,1,0:T(2,128)} %coords_ref.1, bf16[1,128,2,256]{3,2,1,0:T(2,128)(2,1)} %samples_ref.1), custom_call_target="tpu_custom_call" | custom-call | tf_op jit(solution)/shard_map/grid_slots/pallas_call | solution.py:680
  32.6 7.9 %place_slots.1.acc_ref = f32[2,33,192,128]{3,2,1,0:T(8,128)} custom-call(s32[2,8,256]{2,1,0:T(8,128)} %get-tuple-element.8.list_ref, f32[2,8,128]{2,1,0:T(8,128)} %get-tuple-element.9.weight_ref, bf16[32,176,128]{2,1,0:T(8,128)(2,1)} %get-tuple-element.10.pool_ref), custom_call_target="tpu_custom_call" | custom-call | tf_op jit(solution)/shard_map/place_slots/pallas_call | solution.py:710
  40.5 42.2 %swap_rows.1.mixed_ref = bf16[8,512,256]{2,1,0:T(8,128)(2,1)} custom-call(f32[2,33,192,128]{3,2,1,0:T(8,128)} %place_slots.1.acc_ref, f32[16,256]{1,0:T(8,128)} %constant.14.clone.cos_ref, f32[16,256]{1,0:T(8,128)} %constant.15.clone.sin_ref, bf16[512,512]{1,0:T(8,128)(2,1)} %constant.16.clone.second_ref), custom_call_target="tpu_custom_call" | custom-call | tf_op jit(solution)/shard_map/swap_rows/pallas_call | solution.py:725
  82.7 7.3 %image_rows.1 = f32[8,256,256]{2,1,0:T(8,128)} custom-call(s32[1]{0:T(128)} %bitcast.epoch_ref, bf16[8,512,256]{2,1,0:T(8,128)(2,1)} %swap_rows.1.mixed_ref, bf16[16,256,512]{2,1,0:T(8,128)(2,1)} %constant.17.clone.last_ref, f32[8,256]{1,0:T(8,128)} %rows_ref.1, f32[1,256]{1,0:T(1,128)} %bitcast.2), custom_call_target="tpu_custom_call" | custom-call | tf_op jit(solution)/shard_map/image_rows/pallas_call | solution.py:745

commit v4 on v3

--- a/solution.py
+++ b/solution.py
@@ -15,7 +15,7 @@
 FIELDS = 8
 UNROLL = 8
 BEHIND = 3
-VMEM_BYTES = 56 * 1024 * 1024
+VMEM_BYTES = 24 * 1024 * 1024
 MESH = pl.DeviceIdType.MESH
 
 
@@ -108,18 +108,18 @@
 
 def grid_kernel(
     sizes,
-    owner_ref,
-    row_ref,
-    col_ref,
-    coords_ref,
-    samples_ref,
-    pool_ref,
-    list_ref,
-    weight_ref,
-    *scratch,
+    *refs,
 ):
     tile_count, epoch_count, capacity, lane_step, band = sizes
-    packed, points, t_send, t_recv, x_send, x_recv = scratch
+    inputs, (pool_ref, list_ref, weight_ref), scratch = refs[:5], refs[5:8], refs[8:]
+    owner_ref, row_ref, col_ref, coords_ref, samples_ref, in_sem = scratch[:6]
+    packed, points, t_send, t_recv, x_send, x_recv = scratch[6:]
+    fetches = [
+        pltpu.make_async_copy(given, held, in_sem.at[i])
+        for i, (given, held) in enumerate(zip(inputs, scratch))
+    ]
+    for fetch in fetches:
+        fetch.start()
     me, epoch = lax.axis_index("tile"), lax.axis_index("epoch")
     n_slots = owner_ref.shape[1]
     n_samples = coords_ref.shape[3]
@@ -140,6 +140,8 @@
         peer = lax.rem(epoch + k, epoch_count)
         pl.semaphore_signal(barrier, inc=1, device_id={"epoch": peer}, device_id_type=MESH)
 
+    for fetch in fetches:
+        fetch.wait()
     owner = owner_ref[...]
     mirrored = owner >= half
     target = jnp.where(mirrored, 2 * (tile_count - 1 - owner) + 1, 2 * owner)
@@ -377,14 +379,21 @@
         lax.fori_loop(0, (list_ref[e, FIELDS - 1, 0] + UNROLL - 1) // UNROLL, per_batch, 0)
 
 
-def swap_kernel(sizes, cuts, acc_ref, cos_ref, sin_ref, second_ref, mixed_ref, *scratch):
+def swap_kernel(
+    sizes, cuts, acc_ref, cos_ref, sin_ref, second_ref, last_ref, mixed_ref, here_ref, *scratch
+):
     tile_count, epoch_count, band = sizes
+    table_sem, scratch = scratch[0], scratch[1:]
     turned, given, landed, folded, full = scratch[:5]
     p_send, p_recv, t_send, t_recv, x_send, x_recv = scratch[5:]
     me, epoch = lax.axis_index("tile"), lax.axis_index("epoch")
     half, kept = tile_count // 2, tile_count // epoch_count
     mine, side = me // 2, lax.rem(me, 2)
     partner = me + 1 - 2 * side
+    table_copy = pltpu.make_async_copy(
+        last_ref.at[pl.ds(epoch * kept, kept)], here_ref, table_sem.at[0]
+    )
+    table_copy.start()
     rows_here = band // epoch_count
     cut_rows = rows_here // cuts
     width = min(LANES, band)
@@ -596,6 +605,7 @@
             values.append(epoch_turn(value, j + 1, epoch, epoch_count))
         edges.append(dft(values + [None] * (tile_count - half - 1), kept))
     mix_rows(0, 0, 0, edges)
+    table_copy.wait()
 
     for cut in range(cuts):
 
@@ -614,17 +624,16 @@
         lax.fori_loop(0, half, settle, 0)
 
 
-def image_kernel(image_scale, epoch_ref, mixed_ref, last_ref, rows_ref, cols_ref, out_ref, tall):
-    c = pl.program_id(0)
-
-    @pl.when(c == 0)
-    def _():
-        tall[...] = jnp.transpose(rows_ref[...]) * image_scale
-
-    lane = lax.broadcasted_iota(jnp.int32, tall.shape, 1)
-    factor = jnp.sum(jnp.where(lane == c, tall[...], 0.0), 1, keepdims=True)
-    pixels = jnp.dot(last_ref[0], mixed_ref[c], preferred_element_type=jnp.float32)
-    out_ref[0] = pixels * factor * cols_ref[...]
+def image_kernel(image_scale, mixed_ref, last_ref, rows_ref, cols_ref, out_ref, held, sem):
+    kept = held.shape[0]
+    tall = jnp.transpose(rows_ref[...]) * image_scale
+    copies = [pltpu.make_async_copy(held.at[c], out_ref.at[c], sem.at[c]) for c in range(kept)]
+    for c in range(kept):
+        pixels = jnp.dot(last_ref[c], mixed_ref[c], preferred_element_type=jnp.float32)
+        held[c] = pixels * tall[:, c : c + 1] * cols_ref[...]
+        copies[c].start()
+    for c in range(kept):
+        copies[c].wait()
 
 
 def turns(product, modulus):
@@ -653,6 +662,10 @@
     )
 
 
+def hbm(count):
+    return [pl.BlockSpec(memory_space=pltpu.HBM)] * count
+
+
 def vmem(count):
     return [pl.BlockSpec(memory_space=pltpu.VMEM)] * count
 
@@ -670,7 +683,6 @@
     half, kept = tile_count // 2, tile_count // epoch_count
     rows_here = band // epoch_count
     parts = 2 * (band // width)
-    turn_cos, turn_sin, second, last = tables
     sizes = (tile_count, epoch_count, capacity, lane_step, band)
     block_rows = capacity * SUB // 2 + EDGE
     spots = -(-tile_count // (LANES // lane_step)) * LANES
@@ -684,9 +696,14 @@
             jax.ShapeDtypeStruct((epoch_count, FIELDS, spots), jnp.int32),
             jax.ShapeDtypeStruct((epoch_count, FIELDS, LANES), jnp.float32),
         ],
-        in_specs=vmem(5),
+        in_specs=hbm(5),
         out_specs=vmem(3),
         scratch_shapes=[
+            *(
+                pltpu.VMEM(array.shape, array.dtype)
+                for array in (owners, row_offsets, col_offsets, coords, samples)
+            ),
+            pltpu.SemaphoreType.DMA((5,)),
             pltpu.VMEM((tile_count, block_rows, LANES), jnp.bfloat16),
             pltpu.VMEM((tile_count, 2 * lane_step, 2 * n_samples), jnp.float32),
             tile_sems,
@@ -699,11 +716,10 @@
         ),
         name="grid_slots",
     )(
-        owners,
-        row_offsets,
-        col_offsets,
-        coords,
-        samples,
+        *(
+            pltpu.with_memory_space_constraint(array, pltpu.HBM)
+            for array in (owners, row_offsets, col_offsets, coords, samples)
+        )
     )
 
     lane_blocks = tile_count * band // LANES
@@ -722,12 +738,16 @@
     block_shape = (parts * rows_here + EDGE, width)
     sems = [pltpu.SemaphoreType.DMA((cuts * half,))] * 4
     sems += [pltpu.SemaphoreType.DMA((cuts * (epoch_count - 1) * half,))] * 2
-    mixed = pl.pallas_call(
+    mixed, last_here = pl.pallas_call(
         functools.partial(swap_kernel, (tile_count, epoch_count, band), cuts),
-        out_shape=jax.ShapeDtypeStruct((kept, 2 * band, band), jnp.bfloat16),
-        in_specs=vmem(4),
-        out_specs=vmem(1)[0],
+        out_shape=[
+            jax.ShapeDtypeStruct((kept, 2 * band, band), jnp.bfloat16),
+            jax.ShapeDtypeStruct((kept, band, 2 * band), jnp.bfloat16),
+        ],
+        in_specs=vmem(4) + hbm(1),
+        out_specs=vmem(2),
         scratch_shapes=[
+            pltpu.SemaphoreType.DMA((1,)),
             pltpu.VMEM((tile_count, rows_here + EDGE, 2 * band), jnp.bfloat16),
             pltpu.VMEM((half, *block_shape), jnp.bfloat16),
             pltpu.VMEM((half, *block_shape), jnp.bfloat16),
@@ -739,33 +759,21 @@
             vmem_limit_bytes=VMEM_BYTES, collective_id=0, has_side_effects=True
         ),
         name="swap_rows",
-    )(acc, jnp.asarray(turn_cos), jnp.asarray(turn_sin), jnp.asarray(second))
+    )(acc, *(jnp.asarray(table) for table in tables))
 
     image_scale = math.sqrt(n_slots) / (64.0 * tile_count * math.sqrt(epoch_count))
     return pl.pallas_call(
         functools.partial(image_kernel, image_scale),
-        grid_spec=pltpu.PrefetchScalarGridSpec(
-            num_scalar_prefetch=1,
-            grid=(kept,),
-            in_specs=[
-                pl.BlockSpec(memory_space=pltpu.VMEM),
-                pl.BlockSpec((1, band, 2 * band), lambda c, e: (e[0] * kept + c, 0, 0)),
-                pl.BlockSpec((kept, band), lambda c, e: (0, 0)),
-                pl.BlockSpec((1, band), lambda c, e: (0, 0)),
-            ],
-            out_specs=pl.BlockSpec((1, band, band), lambda c, e: (c, 0, 0)),
-            scratch_shapes=[pltpu.VMEM((band, kept), jnp.float32)],
-        ),
         out_shape=jax.ShapeDtypeStruct((kept, band, band), jnp.float32),
+        in_specs=vmem(4),
+        out_specs=hbm(1)[0],
+        scratch_shapes=[
+            pltpu.VMEM((kept, band, band), jnp.float32),
+            pltpu.SemaphoreType.DMA((kept,)),
+        ],
         compiler_params=pltpu.CompilerParams(vmem_limit_bytes=VMEM_BYTES),
         name="image_rows",
-    )(
-        lax.axis_index("epoch").astype(jnp.int32)[None],
-        mixed,
-        jnp.asarray(last),
-        taper_rows,
-        taper_cols[None, :],
-    )
+    )(mixed, last_here, taper_rows, taper_cols[None, :])
 
 
 def solution(mesh):

time: 90 us -> 75.5 us (0.84)
  Pallas kernels: 90 us -> 75.1 us
    pallas_call x1, Pallas kernels: 7.32 us -> 1.72 us  [body(): pl.pallas_call(functools.partial(image_kernel, image_scale), out_shape=ja...]
    pallas_call x1, Pallas kernels: 42.2 us -> 37.1 us  [body(): pl.pallas_call(functools.partial(swap_kernel, (tile_count, epoch_count, b...]
    pallas_call x1, Pallas kernels: 7.88 us -> 5.59 us  [body(): pl.pallas_call(functools.partial(place_kernel, tile_count), out_shape=jax...]
    pallas_call x1, Pallas kernels: 32.6 us -> 30.7 us  [body(): pl.pallas_call(functools.partial(grid_kernel, sizes), out_shape=[jax.Shap...]
where the time goes in v4:
time: 75.5 us; the launch traced here: 75.2 us
  Pallas kernels  75.1 us (99%)
    pallas_call x1, Pallas kernels, body(): pl.pallas_call(functools.partial(swap_kernel, (tile_count, epoch_count, b...  37.1 us
    pallas_call x1, Pallas kernels, body(): pl.pallas_call(functools.partial(grid_kernel, sizes), out_shape=[jax.Shap...  30.7 us
    pallas_call x1, Pallas kernels, body(): pl.pallas_call(functools.partial(place_kernel, tile_count), out_shape=jax...  5.59 us
    pallas_call x1, Pallas kernels, body(): pl.pallas_call(functools.partial(image_kernel, image_scale), out_shape=ja...  1.72 us

profile of v4, /device:TPU:0, one launch (start us, length us, event | category | flops | bytes accessed | tf_op | source)
XLA Modules:
  0.0 75.2 jit_solution(6981958785342323325)
XLA Ops:
  0.0 30.7 %grid_slots.1 = (bf16[32,176,128]{2,1,0:T(8,128)(2,1)S(1)}, s32[2,8,256]{2,1,0:T(8,128)S(1)}, f32[2,8,128]{2,1,0:T(8,128)S(1)}) custom-call(s32[1,128]{1,0:T(1,128)} %refs_0_.1, s32[1,128]{1,0:T(1,128)} %refs_1_.1, s32[1,128]{1,0:T(1,128)} %refs_2_.1, f32[1,128,2,256]{3,2,1,0:T(2,128)} %refs_3_.1, bf16[1,128,2,256]{3,2,1,0:T(2,128)(2,1)} %refs_4_.1), custom_call_target="tpu_custom_call" | custom-call | tf_op jit(solution)/shard_map/grid_slots/pallas_call | solution.py:692
  30.7 0.0 copy-start
  30.7 0.0 copy-start.1
  30.7 0.0 copy-start.2
  30.7 0.0 copy-start.3
  30.7 5.6 %place_slots.1.acc_ref = f32[2,33,192,128]{3,2,1,0:T(8,128)S(1)} custom-call(s32[2,8,256]{2,1,0:T(8,128)S(1)} %get-tuple-element.10.list_ref, f32[2,8,128]{2,1,0:T(8,128)S(1)} %get-tuple-element.11.weight_ref, bf16[32,176,128]{2,1,0:T(8,128)(2,1)S(1)} %get-tuple-element.12.pool_ref), custom_call_target="tpu_custom_call" | custom-call | tf_op jit(solution)/shard_map/place_slots/pallas_call | solution.py:726
  36.3 0.0 copy-done
  36.3 0.0 copy-done.1
  36.3 0.0 copy-done.2
  36.3 0.0 copy-done.3
  36.4 0.0 copy-start.4
  36.4 0.0 copy-start.5
  36.4 37.1 %swap_rows.1 = (bf16[8,512,256]{2,1,0:T(8,128)(2,1)S(1)}, bf16[8,256,512]{2,1,0:T(8,128)(2,1)S(1)}) custom-call(f32[2,33,192,128]{3,2,1,0:T(8,128)S(1)} %place_slots.1.acc_ref, f32[16,256]{1,0:T(8,128)S(1)} %copy-done.3, f32[16,256]{1,0:T(8,128)S(1)} %copy-done.2, bf16[512,512]{1,0:T(8,128)(2,1)S(1)} %copy-done.1, bf16[16,256,512]{2,1,0:T(8,128)(2,1)S(1)} %copy-done), custom_call_target="tpu_custom_call" | custom-call | tf_op jit(solution)/shard_map/swap_rows/pallas_call | solution.py:741
  73.5 0.0 copy-done.4
  73.5 0.0 copy-done.5
  73.5 1.7 %image_rows.1 = f32[8,256,256]{2,1,0:T(8,128)} custom-call(bf16[8,512,256]{2,1,0:T(8,128)(2,1)S(1)} %get-tuple-element.13.mixed_ref, bf16[8,256,512]{2,1,0:T(8,128)(2,1)S(1)} %get-tuple-element.14.last_ref, f32[8,256]{1,0:T(8,128)S(1)} %copy-done.4, f32[1,256]{1,0:T(1,128)S(1)} %bitcast.1), custom_call_target="tpu_custom_call" | custom-call | tf_op jit(solution)/shard_map/image_rows/pallas_call | solution.py:765
Async XLA Ops:
  30.7 5.6 %copy-start = (bf16[16,256,512]{2,1,0:T(8,128)(2,1)S(1)}, bf16[16,256,512]{2,1,0:T(8,128)(2,1)}, u32[]{:S(2)}) copy-start(bf16[16,256,512]{2,1,0:T(8,128)(2,1)} %constant.11.clone.last_ref) | copy-start | bytes 12582916
  30.7 5.6 %copy-start.1 = (bf16[512,512]{1,0:T(8,128)(2,1)S(1)}, bf16[512,512]{1,0:T(8,128)(2,1)}, u32[]{:S(2)}) copy-start(bf16[512,512]{1,0:T(8,128)(2,1)} %constant.10.clone.second_ref) | copy-start | bytes 1572868
  30.7 5.6 %copy-start.2 = (f32[16,256]{1,0:T(8,128)S(1)}, f32[16,256]{1,0:T(8,128)}, u32[]{:S(2)}) copy-start(f32[16,256]{1,0:T(8,128)} %constant.9.clone.sin_ref) | copy-start | bytes 49156
  30.7 5.6 %copy-start.3 = (f32[16,256]{1,0:T(8,128)S(1)}, f32[16,256]{1,0:T(8,128)}, u32[]{:S(2)}) copy-start(f32[16,256]{1,0:T(8,128)} %constant.8.clone.cos_ref) | copy-start | bytes 49156
  36.4 37.1 %copy-start.4 = (f32[8,256]{1,0:T(8,128)S(1)}, f32[8,256]{1,0:T(8,128)}, u32[]{:S(2)}) copy-start(f32[8,256]{1,0:T(8,128)} %rows_ref.1) | copy-start | bytes 24580
  36.4 37.1 %copy-start.5 = (f32[256]{0:T(256)S(1)}, f32[256]{0:T(256)}, u32[]{:S(2)}) copy-start(f32[256]{0:T(256)} %param.17) | copy-start | bytes 3076
